TPU v7x, 32 devices: a whole 2x2x4 slice. The times are simulated.
32 devices in a mesh: sky: 8 (over y, x, core), visit: 4 (over z).
Axes of the slice: x: 2, y: 2, z: 4, core: 2. Of those that a mesh axis runs over, the one named last changes fastest.
Arguments:
- images: bfloat16 [32, 768, 2048], P('visit', 'sky'), may hold values from -6 to 6
- inv_var: bfloat16 [32, 768, 2048], P('visit', 'sky'), may hold values from 0.25 to 4
- row_taps: bfloat16 [11, 41], replicated, may hold values from -1 to 1
- col_taps: bfloat16 [11, 41], replicated, may hold values from -1 to 1
- coeffs: float32 [32, 11, 3], replicated, may hold values from -4 to 4
- dithers: int32 [32], replicated, may hold values from 0 to 256, as said below
- depths: int32 [8], P('sky'), may hold values from 2 to 16, as said below
Outputs:
- coadd: float32 [768, 2048], P('sky', 'visit')
Inputs may be any that keep to these rules, and one draw needn't show every extreme that they name: `dithers`: some visit has offset 0 and some has offset 256. `depths`: some tile is covered by 16 visits.
All inputs are finite; a program needn't handle non-finite values.
Results may differ from a plain program's by a relative error of at most 0.0029.
Values may be sent and summed in bfloat16 or wider, within the bound.
A program may use at most 64 MiB of HBM per device.

v0:
```python
import jax
import jax.numpy as jnp
from jax import lax
from jax.sharding import PartitionSpec as P

DITHER = 256


def extended(cells, sides, width):
    for axis, dim in sides:
        count = lax.axis_size(axis)
        ends = count - 1
        head = lax.slice_in_dim(cells, 0, width, axis=dim)
        tail = lax.slice_in_dim(cells, cells.shape[dim] - width, cells.shape[dim], axis=dim)
        cells = jnp.concatenate(
            [
                lax.ppermute(tail, axis, [(i, (i + 1) % count) for i in range(ends)]),
                cells,
                lax.ppermute(head, axis, [((i + 1) % count, i) for i in range(ends)]),
            ],
            axis=dim,
        )
    return cells


def tap_table(tap_values, out_count, in_count):
    offsets = (
        jnp.arange(in_count, dtype=jnp.int32)[None, :]
        - jnp.arange(out_count, dtype=jnp.int32)[:, None]
    )
    picks = (
        offsets[:, :, None] == jnp.arange(tap_values.shape[1], dtype=jnp.int32)[None, None, :]
    ).astype(jnp.bfloat16)
    return jnp.einsum("kt,oit->koi", tap_values, picks, preferred_element_type=jnp.float32).astype(
        jnp.bfloat16
    )


def batch_terms(
    padded,
    inv_block,
    coef_block,
    offsets,
    covered,
    row_first,
    row_table,
    col_table,
    total_rows,
    total_cols,
):
    visit_count, row_count, col_count = inv_block.shape
    block_count = -(-col_count // 128)
    span_cols = padded.shape[2]
    padded = jnp.pad(padded, ((0, 0), (0, 0), (0, (block_count + 1) * 128 - span_cols)))
    col_ids = jnp.arange(col_count, dtype=jnp.int32)
    row_ids = row_first + jnp.arange(row_count, dtype=jnp.int32)
    col_coord = (2.0 * col_ids.astype(jnp.float32) + 1.0) / total_cols - 1.0
    row_coord = (2.0 * row_ids.astype(jnp.float32) + 1.0) / total_rows - 1.0

    def one_basis(which, matched):
        row_kernel = lax.dynamic_index_in_dim(row_table, which, 0, keepdims=False)
        col_kernel = lax.dynamic_index_in_dim(col_table, which, 0, keepdims=False)
        passed = jnp.einsum(
            "ij,vjx->ivx", row_kernel, padded, preferred_element_type=jnp.float32
        ).astype(jnp.bfloat16)
        pieces = passed.reshape(row_count, visit_count, block_count + 1, 128)
        lower_part = jnp.einsum(
            "rvbj,ij->rvbi", pieces, col_kernel[:, :128], preferred_element_type=jnp.float32
        )
        upper_part = jnp.einsum(
            "rvbj,ij->rvbi", pieces, col_kernel[:, 128:], preferred_element_type=jnp.float32
        )
        basis_image = lower_part[:, :, :-1] + upper_part[:, :, 1:]
        basis_image = basis_image.reshape(row_count, visit_count, block_count * 128)
        coef_now = lax.dynamic_index_in_dim(coef_block, which, 1, keepdims=False)
        spatial = (
            coef_now[None, :, 0, None]
            + coef_now[None, :, 1, None] * col_coord[None, None, :]
            + coef_now[None, :, 2, None] * row_coord[:, None, None]
        )
        return matched + spatial * basis_image

    starting = jnp.zeros((row_count, visit_count, col_count), jnp.float32)
    matched = lax.fori_loop(0, row_table.shape[0], one_basis, starting)
    inside = (col_ids[None, :] >= offsets[:, None]) & (
        col_ids[None, :] < offsets[:, None] + total_cols - DITHER
    )
    weight = (
        inv_block.astype(jnp.float32)
        * inside[:, None, :].astype(jnp.float32)
        * covered[:, None, None].astype(jnp.float32)
    )
    weight = jnp.transpose(weight, (1, 0, 2))
    return (jnp.sum(weight * matched, axis=1), jnp.sum(weight, axis=1))


def local(images, inv_var, row_taps, col_taps, coeffs, dithers, depths):
    visit_count, row_count, col_count = images.shape
    half_taps = row_taps.shape[1] // 2
    sky_index = lax.axis_index("sky")
    tile_count = lax.axis_size("sky")
    group_index = lax.axis_index("visit")
    group_count = lax.axis_size("visit")
    visits_all = visit_count * group_count
    first_visit = sky_index * visits_all // tile_count
    tile_depth = depths[0]
    total_rows = row_count * tile_count
    row_first = sky_index * row_count
    row_table = tap_table(row_taps, row_count, row_count + 2 * half_taps)
    col_table = tap_table(col_taps, 128, 256)
    padded = extended(images, (("sky", 1),), half_taps)
    padded = jnp.pad(padded, ((0, 0), (0, 0), (half_taps, half_taps)))
    visit_order = group_index * visit_count + jnp.arange(visit_count, dtype=jnp.int32)
    covered = jnp.mod(visit_order - first_visit, visits_all) < tile_depth
    coef_block = lax.dynamic_slice_in_dim(coeffs, group_index * visit_count, visit_count, 0)
    offsets = lax.dynamic_slice_in_dim(dithers, group_index * visit_count, visit_count, 0)
    partial_value = batch_terms(
        padded,
        inv_var,
        coef_block,
        offsets,
        covered,
        row_first,
        row_table,
        col_table,
        total_rows,
        col_count,
    )
    numerator, denominator = (
        lax.psum_scatter(partial_value[0], "visit", scatter_dimension=1, tiled=True),
        lax.psum_scatter(partial_value[1], "visit", scatter_dimension=1, tiled=True),
    )
    return numerator / (1.0 + denominator)


def solution(mesh):
    placed = (P("visit", "sky", None), P("visit", "sky", None), P(), P(), P(), P(), P("sky"))
    return jax.shard_map(
        local, mesh=mesh, in_specs=placed, out_specs=P("sky", "visit"), check_vma=False
    )
```

profile of v0, /device:TPU:1, one launch (start us, length us, event | category | flops | bytes accessed | tf_op | source)
XLA Modules:
  0.0 303.2 jit_solution(4412814811402359373)
XLA Ops:
  12.6 4.5 %collective-permute-start = (bf16[8,20,2048]{2,0,1:T(8,128)(2,1)}, bf16[8,20,2048]{2,0,1:T(8,128)(2,1)}, u32[]{:S(2)}, u32[]{:S(2)}) collective-permute-start(bf16[8,20,2048]{2,0,1:T(8,128)(2,1)} %copy.27), channel_id=1, source_target_pairs={{0,4},{4,8},{8,12},{12,16},{16,20},{20,24},{24,28},{1,5},{5,9},{9,... | collective-permute-start | bytes 1966088 | tf_op jit(solution)/shard_map/ppermute | solution.py:17
  28.2 4.0 %fusion.23 = bf16[8,136,2088]{2,1,0:T(8,128)(2,1)S(1)} fusion(bf16[8,20,2048]{2,1,0:T(8,128)(2,1)S(1)} %copy.22, bf16[8,96,2048]{2,1,0:T(8,128)(2,1)S(1)} %copy-done.2, bf16[8,20,2048]{2,1,0:T(8,128)(2,1)S(1)} %copy.21), kind=kLoop, calls=%fused_computation.38 | loop fusion | flops 27260928 | bytes 8999936 | tf_op jit(solution)/shard_map/concatenate | solution.py:15
  34.8 199.8 %while.14 = (s32[]{:T(128)}, f32[96,8,2048]{2,1,0:T(8,128)}, f32[8,11,3]{0,2,1:T(4,128)}, bf16[11,96,136]{1,2,0:T(8,128)(2,1)S(1)}, bf16[8,136,2176]{2,1,0:T(8,1...) while((s32[]{:T(128)}, f32[96,8,2048]{2,1,0:T(8,128)}, ...), condition=%wide.region_1.2_spmd.clone, body=%wide.region_0.1_spmd.clone.sunk | while | flops 1269443840 | bytes 84400552 | solution.py:84
  40.2 3.9 %fusion.48 = f32[96,8,16,128]{3,1,2,0:T(8,128)S(1)} fusion(bf16[96,8,2176]{2,0,1:T(8,128)(2,1)S(1)} %convolution_convert_fusion.2, bf16[128,256]{1,0:T(8,128)(2,1)S(1)} %dynamic-slice_bitcast_fusion.4), kind=kOutput, calls=%fused_computation.5.clone.1 | convolution fusion | flops 402653184 | bytes 9666560 | tf_op jit(solution)/shard_map/while/body/eval_jaxpr/slice | solution.py:73
  44.2 6.2 %fusion.49 = f32[96,8,2048]{2,1,0:T(8,128)S(1)} fusion(f32[96,8,2048]{2,1,0:T(8,128)S(1)} %bitcast.74, f32[96,8,16,128]{3,1,2,0:T(8,128)S(1)} %fusion.48, f32[96,8]{1,0:T(8,128)S(1)} %broadcast_multiply_fusion.2, f32[8,2048]{1,0:T(8,128)S(1)} %multiply_add_fusion.8, pred[]{:T(512)S(6)} %compare.51, ...), kind=kOutput, calls=%fused_computation.3.clone.1 | convolution fusion | flops 410517504 | bytes 22364160 | tf_op jit(solution)/shard_map/while/body/eval_jaxpr/slice | solution.py:73
  58.4 3.9 %fusion.48 = f32[96,8,16,128]{3,1,2,0:T(8,128)S(1)} fusion(bf16[96,8,2176]{2,0,1:T(8,128)(2,1)S(1)} %convolution_convert_fusion.2, bf16[128,256]{1,0:T(8,128)(2,1)S(1)} %dynamic-slice_bitcast_fusion.4), kind=kOutput, calls=%fused_computation.5.clone.1 | convolution fusion | flops 402653184 | bytes 9666560 | tf_op jit(solution)/shard_map/while/body/eval_jaxpr/slice | solution.py:73
  62.4 6.2 %fusion.49 = f32[96,8,2048]{2,1,0:T(8,128)S(1)} fusion(f32[96,8,2048]{2,1,0:T(8,128)S(1)} %bitcast.74, f32[96,8,16,128]{3,1,2,0:T(8,128)S(1)} %fusion.48, f32[96,8]{1,0:T(8,128)S(1)} %broadcast_multiply_fusion.2, f32[8,2048]{1,0:T(8,128)S(1)} %multiply_add_fusion.8, pred[]{:T(512)S(6)} %compare.51, ...), kind=kOutput, calls=%fused_computation.3.clone.1 | convolution fusion | flops 410517504 | bytes 22364160 | tf_op jit(solution)/shard_map/while/body/eval_jaxpr/slice | solution.py:73
  76.5 3.9 %fusion.48 = f32[96,8,16,128]{3,1,2,0:T(8,128)S(1)} fusion(bf16[96,8,2176]{2,0,1:T(8,128)(2,1)S(1)} %convolution_convert_fusion.2, bf16[128,256]{1,0:T(8,128)(2,1)S(1)} %dynamic-slice_bitcast_fusion.4), kind=kOutput, calls=%fused_computation.5.clone.1 | convolution fusion | flops 402653184 | bytes 9666560 | tf_op jit(solution)/shard_map/while/body/eval_jaxpr/slice | solution.py:73
  80.5 6.2 %fusion.49 = f32[96,8,2048]{2,1,0:T(8,128)S(1)} fusion(f32[96,8,2048]{2,1,0:T(8,128)S(1)} %bitcast.74, f32[96,8,16,128]{3,1,2,0:T(8,128)S(1)} %fusion.48, f32[96,8]{1,0:T(8,128)S(1)} %broadcast_multiply_fusion.2, f32[8,2048]{1,0:T(8,128)S(1)} %multiply_add_fusion.8, pred[]{:T(512)S(6)} %compare.51, ...), kind=kOutput, calls=%fused_computation.3.clone.1 | convolution fusion | flops 410517504 | bytes 22364160 | tf_op jit(solution)/shard_map/while/body/eval_jaxpr/slice | solution.py:73
  94.7 3.9 %fusion.48 = f32[96,8,16,128]{3,1,2,0:T(8,128)S(1)} fusion(bf16[96,8,2176]{2,0,1:T(8,128)(2,1)S(1)} %convolution_convert_fusion.2, bf16[128,256]{1,0:T(8,128)(2,1)S(1)} %dynamic-slice_bitcast_fusion.4), kind=kOutput, calls=%fused_computation.5.clone.1 | convolution fusion | flops 402653184 | bytes 9666560 | tf_op jit(solution)/shard_map/while/body/eval_jaxpr/slice | solution.py:73
  98.7 6.2 %fusion.49 = f32[96,8,2048]{2,1,0:T(8,128)S(1)} fusion(f32[96,8,2048]{2,1,0:T(8,128)S(1)} %bitcast.74, f32[96,8,16,128]{3,1,2,0:T(8,128)S(1)} %fusion.48, f32[96,8]{1,0:T(8,128)S(1)} %broadcast_multiply_fusion.2, f32[8,2048]{1,0:T(8,128)S(1)} %multiply_add_fusion.8, pred[]{:T(512)S(6)} %compare.51, ...), kind=kOutput, calls=%fused_computation.3.clone.1 | convolution fusion | flops 410517504 | bytes 22364160 | tf_op jit(solution)/shard_map/while/body/eval_jaxpr/slice | solution.py:73
  109.2 3.6 %convolution_convert_fusion.2 = bf16[96,8,2176]{2,0,1:T(8,128)(2,1)S(1)} fusion(bf16[8,136,2176]{2,1,0:T(8,128)(2,1)} %get-tuple-element.289, bf16[11,96,136]{1,2,0:T(8,128)(2,1)S(1)} %get-tuple-element.288, s32[]{:T(128)S(6)} %copy.47), kind=kOutput, calls=%fused_computation.4.clone.1 | convolution fusion | flops 456228864 | bytes 8112132 | tf_op jit(solution)/shard_map/while/body/eval_jaxpr/ij,vjx->ivx/dot_general | solution.py:63
  112.8 3.9 %fusion.48 = f32[96,8,16,128]{3,1,2,0:T(8,128)S(1)} fusion(bf16[96,8,2176]{2,0,1:T(8,128)(2,1)S(1)} %convolution_convert_fusion.2, bf16[128,256]{1,0:T(8,128)(2,1)S(1)} %dynamic-slice_bitcast_fusion.4), kind=kOutput, calls=%fused_computation.5.clone.1 | convolution fusion | flops 402653184 | bytes 9666560 | tf_op jit(solution)/shard_map/while/body/eval_jaxpr/slice | solution.py:73
  116.8 6.2 %fusion.49 = f32[96,8,2048]{2,1,0:T(8,128)S(1)} fusion(f32[96,8,2048]{2,1,0:T(8,128)S(1)} %bitcast.74, f32[96,8,16,128]{3,1,2,0:T(8,128)S(1)} %fusion.48, f32[96,8]{1,0:T(8,128)S(1)} %broadcast_multiply_fusion.2, f32[8,2048]{1,0:T(8,128)S(1)} %multiply_add_fusion.8, pred[]{:T(512)S(6)} %compare.51, ...), kind=kOutput, calls=%fused_computation.3.clone.1 | convolution fusion | flops 410517504 | bytes 22364160 | tf_op jit(solution)/shard_map/while/body/eval_jaxpr/slice | solution.py:73
  127.4 3.6 %convolution_convert_fusion.2 = bf16[96,8,2176]{2,0,1:T(8,128)(2,1)S(1)} fusion(bf16[8,136,2176]{2,1,0:T(8,128)(2,1)} %get-tuple-element.289, bf16[11,96,136]{1,2,0:T(8,128)(2,1)S(1)} %get-tuple-element.288, s32[]{:T(128)S(6)} %copy.47), kind=kOutput, calls=%fused_computation.4.clone.1 | convolution fusion | flops 456228864 | bytes 8112132 | tf_op jit(solution)/shard_map/while/body/eval_jaxpr/ij,vjx->ivx/dot_general | solution.py:63
  131.0 3.9 %fusion.48 = f32[96,8,16,128]{3,1,2,0:T(8,128)S(1)} fusion(bf16[96,8,2176]{2,0,1:T(8,128)(2,1)S(1)} %convolution_convert_fusion.2, bf16[128,256]{1,0:T(8,128)(2,1)S(1)} %dynamic-slice_bitcast_fusion.4), kind=kOutput, calls=%fused_computation.5.clone.1 | convolution fusion | flops 402653184 | bytes 9666560 | tf_op jit(solution)/shard_map/while/body/eval_jaxpr/slice | solution.py:73
  134.9 6.2 %fusion.49 = f32[96,8,2048]{2,1,0:T(8,128)S(1)} fusion(f32[96,8,2048]{2,1,0:T(8,128)S(1)} %bitcast.74, f32[96,8,16,128]{3,1,2,0:T(8,128)S(1)} %fusion.48, f32[96,8]{1,0:T(8,128)S(1)} %broadcast_multiply_fusion.2, f32[8,2048]{1,0:T(8,128)S(1)} %multiply_add_fusion.8, pred[]{:T(512)S(6)} %compare.51, ...), kind=kOutput, calls=%fused_computation.3.clone.1 | convolution fusion | flops 410517504 | bytes 22364160 | tf_op jit(solution)/shard_map/while/body/eval_jaxpr/slice | solution.py:73
  145.5 3.6 %convolution_convert_fusion.2 = bf16[96,8,2176]{2,0,1:T(8,128)(2,1)S(1)} fusion(bf16[8,136,2176]{2,1,0:T(8,128)(2,1)} %get-tuple-element.289, bf16[11,96,136]{1,2,0:T(8,128)(2,1)S(1)} %get-tuple-element.288, s32[]{:T(128)S(6)} %copy.47), kind=kOutput, calls=%fused_computation.4.clone.1 | convolution fusion | flops 456228864 | bytes 8112132 | tf_op jit(solution)/shard_map/while/body/eval_jaxpr/ij,vjx->ivx/dot_general | solution.py:63
  149.1 3.9 %fusion.48 = f32[96,8,16,128]{3,1,2,0:T(8,128)S(1)} fusion(bf16[96,8,2176]{2,0,1:T(8,128)(2,1)S(1)} %convolution_convert_fusion.2, bf16[128,256]{1,0:T(8,128)(2,1)S(1)} %dynamic-slice_bitcast_fusion.4), kind=kOutput, calls=%fused_computation.5.clone.1 | convolution fusion | flops 402653184 | bytes 9666560 | tf_op jit(solution)/shard_map/while/body/eval_jaxpr/slice | solution.py:73
  153.1 6.2 %fusion.49 = f32[96,8,2048]{2,1,0:T(8,128)S(1)} fusion(f32[96,8,2048]{2,1,0:T(8,128)S(1)} %bitcast.74, f32[96,8,16,128]{3,1,2,0:T(8,128)S(1)} %fusion.48, f32[96,8]{1,0:T(8,128)S(1)} %broadcast_multiply_fusion.2, f32[8,2048]{1,0:T(8,128)S(1)} %multiply_add_fusion.8, pred[]{:T(512)S(6)} %compare.51, ...), kind=kOutput, calls=%fused_computation.3.clone.1 | convolution fusion | flops 410517504 | bytes 22364160 | tf_op jit(solution)/shard_map/while/body/eval_jaxpr/slice | solution.py:73
  163.7 3.6 %convolution_convert_fusion.2 = bf16[96,8,2176]{2,0,1:T(8,128)(2,1)S(1)} fusion(bf16[8,136,2176]{2,1,0:T(8,128)(2,1)} %get-tuple-element.289, bf16[11,96,136]{1,2,0:T(8,128)(2,1)S(1)} %get-tuple-element.288, s32[]{:T(128)S(6)} %copy.47), kind=kOutput, calls=%fused_computation.4.clone.1 | convolution fusion | flops 456228864 | bytes 8112132 | tf_op jit(solution)/shard_map/while/body/eval_jaxpr/ij,vjx->ivx/dot_general | solution.py:63
  167.3 3.9 %fusion.48 = f32[96,8,16,128]{3,1,2,0:T(8,128)S(1)} fusion(bf16[96,8,2176]{2,0,1:T(8,128)(2,1)S(1)} %convolution_convert_fusion.2, bf16[128,256]{1,0:T(8,128)(2,1)S(1)} %dynamic-slice_bitcast_fusion.4), kind=kOutput, calls=%fused_computation.5.clone.1 | convolution fusion | flops 402653184 | bytes 9666560 | tf_op jit(solution)/shard_map/while/body/eval_jaxpr/slice | solution.py:73
  171.3 6.2 %fusion.49 = f32[96,8,2048]{2,1,0:T(8,128)S(1)} fusion(f32[96,8,2048]{2,1,0:T(8,128)S(1)} %bitcast.74, f32[96,8,16,128]{3,1,2,0:T(8,128)S(1)} %fusion.48, f32[96,8]{1,0:T(8,128)S(1)} %broadcast_multiply_fusion.2, f32[8,2048]{1,0:T(8,128)S(1)} %multiply_add_fusion.8, pred[]{:T(512)S(6)} %compare.51, ...), kind=kOutput, calls=%fused_computation.3.clone.1 | convolution fusion | flops 410517504 | bytes 22364160 | tf_op jit(solution)/shard_map/while/body/eval_jaxpr/slice | solution.py:73
  185.5 3.9 %fusion.48 = f32[96,8,16,128]{3,1,2,0:T(8,128)S(1)} fusion(bf16[96,8,2176]{2,0,1:T(8,128)(2,1)S(1)} %convolution_convert_fusion.2, bf16[128,256]{1,0:T(8,128)(2,1)S(1)} %dynamic-slice_bitcast_fusion.4), kind=kOutput, calls=%fused_computation.5.clone.1 | convolution fusion | flops 402653184 | bytes 9666560 | tf_op jit(solution)/shard_map/while/body/eval_jaxpr/slice | solution.py:73
  189.4 6.2 %fusion.49 = f32[96,8,2048]{2,1,0:T(8,128)S(1)} fusion(f32[96,8,2048]{2,1,0:T(8,128)S(1)} %bitcast.74, f32[96,8,16,128]{3,1,2,0:T(8,128)S(1)} %fusion.48, f32[96,8]{1,0:T(8,128)S(1)} %broadcast_multiply_fusion.2, f32[8,2048]{1,0:T(8,128)S(1)} %multiply_add_fusion.8, pred[]{:T(512)S(6)} %compare.51, ...), kind=kOutput, calls=%fused_computation.3.clone.1 | convolution fusion | flops 410517504 | bytes 22364160 | tf_op jit(solution)/shard_map/while/body/eval_jaxpr/slice | solution.py:73
  203.6 3.9 %fusion.48 = f32[96,8,16,128]{3,1,2,0:T(8,128)S(1)} fusion(bf16[96,8,2176]{2,0,1:T(8,128)(2,1)S(1)} %convolution_convert_fusion.2, bf16[128,256]{1,0:T(8,128)(2,1)S(1)} %dynamic-slice_bitcast_fusion.4), kind=kOutput, calls=%fused_computation.5.clone.1 | convolution fusion | flops 402653184 | bytes 9666560 | tf_op jit(solution)/shard_map/while/body/eval_jaxpr/slice | solution.py:73
  207.5 6.2 %fusion.49 = f32[96,8,2048]{2,1,0:T(8,128)S(1)} fusion(f32[96,8,2048]{2,1,0:T(8,128)S(1)} %bitcast.74, f32[96,8,16,128]{3,1,2,0:T(8,128)S(1)} %fusion.48, f32[96,8]{1,0:T(8,128)S(1)} %broadcast_multiply_fusion.2, f32[8,2048]{1,0:T(8,128)S(1)} %multiply_add_fusion.8, pred[]{:T(512)S(6)} %compare.51, ...), kind=kOutput, calls=%fused_computation.3.clone.1 | convolution fusion | flops 410517504 | bytes 22364160 | tf_op jit(solution)/shard_map/while/body/eval_jaxpr/slice | solution.py:73
  221.7 3.9 %fusion.48 = f32[96,8,16,128]{3,1,2,0:T(8,128)S(1)} fusion(bf16[96,8,2176]{2,0,1:T(8,128)(2,1)S(1)} %convolution_convert_fusion.2, bf16[128,256]{1,0:T(8,128)(2,1)S(1)} %dynamic-slice_bitcast_fusion.4), kind=kOutput, calls=%fused_computation.5.clone.1 | convolution fusion | flops 402653184 | bytes 9666560 | tf_op jit(solution)/shard_map/while/body/eval_jaxpr/slice | solution.py:73
  225.7 6.2 %fusion.49 = f32[96,8,2048]{2,1,0:T(8,128)S(1)} fusion(f32[96,8,2048]{2,1,0:T(8,128)S(1)} %bitcast.74, f32[96,8,16,128]{3,1,2,0:T(8,128)S(1)} %fusion.48, f32[96,8]{1,0:T(8,128)S(1)} %broadcast_multiply_fusion.2, f32[8,2048]{1,0:T(8,128)S(1)} %multiply_add_fusion.8, pred[]{:T(512)S(6)} %compare.51, ...), kind=kOutput, calls=%fused_computation.3.clone.1 | convolution fusion | flops 410517504 | bytes 22364160 | tf_op jit(solution)/shard_map/while/body/eval_jaxpr/slice | solution.py:73
  234.6 9.0 %bitcast_reduce_fusion = (f32[96,2048]{1,0:T(8,128)}, f32[96,2048]{1,0:T(8,128)}) fusion(f32[8]{0:T(128)} %compare_convert_fusion, f32[8,2048]{1,0:T(8,128)} %fusion.32, bf16[8,96,2048]{2,1,0:T(8,128)(2,1)S(1)} %copy-done.3, f32[96,8,2048]{2,1,0:T(8,128)} %get-tuple-element.144), kind=kLoop, calls=%fused_computation.28 | loop fusion | flops 9043968 | bytes 11075616 | tf_op jit(solution)/shard_map/reduce_sum | solution.py:94
  244.4 25.3 %reduce-scatter.5.cloned.1.call-done = f32[96,512]{1,0:T(8,128)} async-done(((f32[96,2048]{1,0:T(8,128)}), f32[96,512]{1,0:T(8,128)}) %reduce-scatter.5.cloned.1.call-update) | async-done | bytes 196624 | tf_op jit(solution)/shard_map/reduce_scatter | solution.py:131
  269.7 24.9 %reduce-scatter.3.cloned.1.call-done = f32[96,512]{1,0:T(8,128)} async-done(((f32[96,2048]{1,0:T(8,128)}), f32[96,512]{1,0:T(8,128)}) %reduce-scatter.3.cloned.1.call-update) | async-done | bytes 196624 | tf_op jit(solution)/shard_map/reduce_scatter | solution.py:130
  (194 shorter events, 94.5 us)
Async XLA Ops:
  6.5 17.3 %copy-start = (f32[32,11,3]{0,2,1:T(4,128)S(1)}, f32[32,11,3]{0,2,1:T(4,128)}, u32[]{:S(2)}) copy-start(f32[32,11,3]{0,2,1:T(4,128)} %param.13) | copy-start | bytes 12676
  6.5 11.8 %copy-start.4 = (bf16[11,41]{1,0:T(8,128)(2,1)S(1)}, bf16[11,41]{1,0:T(8,128)(2,1)}, u32[]{:S(2)}) copy-start(bf16[11,41]{1,0:T(8,128)(2,1)} %param.11) | copy-start | bytes 2710
  6.5 263.2 %reduce-scatter.5.cloned.1.call-start = ((), (), s32[]{:S(2)}) async-start(), calls=%async_computation.3 | async-start | bytes 983040 | tf_op jit(solution)/shard_map/reduce_scatter | solution.py:131
  9.4 15.9 %collective-permute-start.1 = (bf16[8,20,2048]{2,0,1:T(8,128)(2,1)}, bf16[8,20,2048]{2,0,1:T(8,128)(2,1)}, u32[]{:S(2)}, u32[]{:S(2)}) collective-permute-start(bf16[8,20,2048]{2,0,1:T(8,128)(2,1)} %copy.28), channel_id=1, source_target_pairs={{4,0},{8,4},{12,8},{16,12},{20,16},{24,20},{28,24},{5,1},{9,5},{13... | collective-permute-start | bytes 1966088 | tf_op jit(solution)/shard_map/ppermute | solution.py:19
  11.3 16.9 %copy-start.2 = (bf16[8,96,2048]{2,1,0:T(8,128)(2,1)S(1)}, bf16[8,96,2048]{2,1,0:T(8,128)(2,1)}, u32[]{:S(2)}) copy-start(bf16[8,96,2048]{2,1,0:T(8,128)(2,1)} %param.9) | copy-start | bytes 9437188
  12.6 14.1 %collective-permute-start = (bf16[8,20,2048]{2,0,1:T(8,128)(2,1)}, bf16[8,20,2048]{2,0,1:T(8,128)(2,1)}, u32[]{:S(2)}, u32[]{:S(2)}) collective-permute-start(bf16[8,20,2048]{2,0,1:T(8,128)(2,1)} %copy.27), channel_id=1, source_target_pairs={{0,4},{4,8},{8,12},{12,16},{16,20},{20,24},{24,28},{1,5},{5,9},{9,... | collective-permute-start | bytes 1966088 | tf_op jit(solution)/shard_map/ppermute | solution.py:17
  34.8 199.8 %copy-start.3 = (bf16[8,96,2048]{2,1,0:T(8,128)(2,1)S(1)}, bf16[8,96,2048]{2,1,0:T(8,128)(2,1)}, u32[]{:S(2)}) copy-start(bf16[8,96,2048]{2,1,0:T(8,128)(2,1)} %param.10) | copy-start | bytes 9437188
  36.6 7.5 %slice-start = ((s8[6291456]{0:T(1024)(128)(4,1)}), s8[4194304]{0:T(1024)(128)(4,1)S(1)}, s32[]{:S(2)}) async-start(s8[6291456]{0:T(1024)(128)(4,1)} %bitcast.73), calls=%async_computation.4 | async-start | bytes 8388608 | tf_op jit(solution)/shard_map/while
  40.2 4.0 %slice-start.1 = ((s8[6291456]{0:T(1024)(128)(4,1)}), s8[2097152]{0:T(1024)(128)(4,1)S(1)}, s32[]{:S(2)}) async-start(s8[6291456]{0:T(1024)(128)(4,1)} %bitcast.73), calls=%async_computation.5 | async-start | bytes 4194304 | tf_op jit(solution)/shard_map/while
  50.4 2.7 copy-start.1
  54.8 7.5 %slice-start = ((s8[6291456]{0:T(1024)(128)(4,1)}), s8[4194304]{0:T(1024)(128)(4,1)S(1)}, s32[]{:S(2)}) async-start(s8[6291456]{0:T(1024)(128)(4,1)} %bitcast.73), calls=%async_computation.4 | async-start | bytes 8388608 | tf_op jit(solution)/shard_map/while
  58.4 4.0 %slice-start.1 = ((s8[6291456]{0:T(1024)(128)(4,1)}), s8[2097152]{0:T(1024)(128)(4,1)S(1)}, s32[]{:S(2)}) async-start(s8[6291456]{0:T(1024)(128)(4,1)} %bitcast.73), calls=%async_computation.5 | async-start | bytes 4194304 | tf_op jit(solution)/shard_map/while
  72.9 7.5 %slice-start = ((s8[6291456]{0:T(1024)(128)(4,1)}), s8[4194304]{0:T(1024)(128)(4,1)S(1)}, s32[]{:S(2)}) async-start(s8[6291456]{0:T(1024)(128)(4,1)} %bitcast.73), calls=%async_computation.4 | async-start | bytes 8388608 | tf_op jit(solution)/shard_map/while
  76.5 4.0 %slice-start.1 = ((s8[6291456]{0:T(1024)(128)(4,1)}), s8[2097152]{0:T(1024)(128)(4,1)S(1)}, s32[]{:S(2)}) async-start(s8[6291456]{0:T(1024)(128)(4,1)} %bitcast.73), calls=%async_computation.5 | async-start | bytes 4194304 | tf_op jit(solution)/shard_map/while
  91.1 7.5 %slice-start = ((s8[6291456]{0:T(1024)(128)(4,1)}), s8[4194304]{0:T(1024)(128)(4,1)S(1)}, s32[]{:S(2)}) async-start(s8[6291456]{0:T(1024)(128)(4,1)} %bitcast.73), calls=%async_computation.4 | async-start | bytes 8388608 | tf_op jit(solution)/shard_map/while
  94.7 4.0 %slice-start.1 = ((s8[6291456]{0:T(1024)(128)(4,1)}), s8[2097152]{0:T(1024)(128)(4,1)S(1)}, s32[]{:S(2)}) async-start(s8[6291456]{0:T(1024)(128)(4,1)} %bitcast.73), calls=%async_computation.5 | async-start | bytes 4194304 | tf_op jit(solution)/shard_map/while
  104.9 2.7 copy-start.1
  109.2 7.6 %slice-start = ((s8[6291456]{0:T(1024)(128)(4,1)}), s8[4194304]{0:T(1024)(128)(4,1)S(1)}, s32[]{:S(2)}) async-start(s8[6291456]{0:T(1024)(128)(4,1)} %bitcast.73), calls=%async_computation.4 | async-start | bytes 8388608 | tf_op jit(solution)/shard_map/while
  112.8 4.0 %slice-start.1 = ((s8[6291456]{0:T(1024)(128)(4,1)}), s8[2097152]{0:T(1024)(128)(4,1)S(1)}, s32[]{:S(2)}) async-start(s8[6291456]{0:T(1024)(128)(4,1)} %bitcast.73), calls=%async_computation.5 | async-start | bytes 4194304 | tf_op jit(solution)/shard_map/while
  127.4 7.6 %slice-start = ((s8[6291456]{0:T(1024)(128)(4,1)}), s8[4194304]{0:T(1024)(128)(4,1)S(1)}, s32[]{:S(2)}) async-start(s8[6291456]{0:T(1024)(128)(4,1)} %bitcast.73), calls=%async_computation.4 | async-start | bytes 8388608 | tf_op jit(solution)/shard_map/while
  131.0 4.0 %slice-start.1 = ((s8[6291456]{0:T(1024)(128)(4,1)}), s8[2097152]{0:T(1024)(128)(4,1)S(1)}, s32[]{:S(2)}) async-start(s8[6291456]{0:T(1024)(128)(4,1)} %bitcast.73), calls=%async_computation.5 | async-start | bytes 4194304 | tf_op jit(solution)/shard_map/while
  145.5 7.6 %slice-start = ((s8[6291456]{0:T(1024)(128)(4,1)}), s8[4194304]{0:T(1024)(128)(4,1)S(1)}, s32[]{:S(2)}) async-start(s8[6291456]{0:T(1024)(128)(4,1)} %bitcast.73), calls=%async_computation.4 | async-start | bytes 8388608 | tf_op jit(solution)/shard_map/while
  149.1 4.0 %slice-start.1 = ((s8[6291456]{0:T(1024)(128)(4,1)}), s8[2097152]{0:T(1024)(128)(4,1)S(1)}, s32[]{:S(2)}) async-start(s8[6291456]{0:T(1024)(128)(4,1)} %bitcast.73), calls=%async_computation.5 | async-start | bytes 4194304 | tf_op jit(solution)/shard_map/while
  163.7 7.6 %slice-start = ((s8[6291456]{0:T(1024)(128)(4,1)}), s8[4194304]{0:T(1024)(128)(4,1)S(1)}, s32[]{:S(2)}) async-start(s8[6291456]{0:T(1024)(128)(4,1)} %bitcast.73), calls=%async_computation.4 | async-start | bytes 8388608 | tf_op jit(solution)/shard_map/while
  167.3 4.0 %slice-start.1 = ((s8[6291456]{0:T(1024)(128)(4,1)}), s8[2097152]{0:T(1024)(128)(4,1)S(1)}, s32[]{:S(2)}) async-start(s8[6291456]{0:T(1024)(128)(4,1)} %bitcast.73), calls=%async_computation.5 | async-start | bytes 4194304 | tf_op jit(solution)/shard_map/while
  181.9 7.5 %slice-start = ((s8[6291456]{0:T(1024)(128)(4,1)}), s8[4194304]{0:T(1024)(128)(4,1)S(1)}, s32[]{:S(2)}) async-start(s8[6291456]{0:T(1024)(128)(4,1)} %bitcast.73), calls=%async_computation.4 | async-start | bytes 8388608 | tf_op jit(solution)/shard_map/while
  185.4 4.0 %slice-start.1 = ((s8[6291456]{0:T(1024)(128)(4,1)}), s8[2097152]{0:T(1024)(128)(4,1)S(1)}, s32[]{:S(2)}) async-start(s8[6291456]{0:T(1024)(128)(4,1)} %bitcast.73), calls=%async_computation.5 | async-start | bytes 4194304 | tf_op jit(solution)/shard_map/while
  200.0 7.5 %slice-start = ((s8[6291456]{0:T(1024)(128)(4,1)}), s8[4194304]{0:T(1024)(128)(4,1)S(1)}, s32[]{:S(2)}) async-start(s8[6291456]{0:T(1024)(128)(4,1)} %bitcast.73), calls=%async_computation.4 | async-start | bytes 8388608 | tf_op jit(solution)/shard_map/while
  203.5 4.0 %slice-start.1 = ((s8[6291456]{0:T(1024)(128)(4,1)}), s8[2097152]{0:T(1024)(128)(4,1)S(1)}, s32[]{:S(2)}) async-start(s8[6291456]{0:T(1024)(128)(4,1)} %bitcast.73), calls=%async_computation.5 | async-start | bytes 4194304 | tf_op jit(solution)/shard_map/while
  218.1 7.6 %slice-start = ((s8[6291456]{0:T(1024)(128)(4,1)}), s8[4194304]{0:T(1024)(128)(4,1)S(1)}, s32[]{:S(2)}) async-start(s8[6291456]{0:T(1024)(128)(4,1)} %bitcast.73), calls=%async_computation.4 | async-start | bytes 8388608 | tf_op jit(solution)/shard_map/while
  221.7 4.0 %slice-start.1 = ((s8[6291456]{0:T(1024)(128)(4,1)}), s8[2097152]{0:T(1024)(128)(4,1)S(1)}, s32[]{:S(2)}) async-start(s8[6291456]{0:T(1024)(128)(4,1)} %bitcast.73), calls=%async_computation.5 | async-start | bytes 4194304 | tf_op jit(solution)/shard_map/while
  243.6 51.0 %reduce-scatter.3.cloned.1.call-start = ((), (), s32[]{:S(2)}) async-start(), calls=%async_computation.2 | async-start | bytes 983040 | tf_op jit(solution)/shard_map/reduce_scatter | solution.py:130
  (9 other events, 24.0 us)
Sparse Core Ops, SparseCore 0:
  243.8 25.9 reduce-scatter.4
  272.0 22.5 reduce-scatter.2
where the time goes:
time: 306 us; the launch traced here: 303 us
  matrix products  154 us (50%)
  local copies, waits for them, and re-layouts  57.5 us (19%)
  waiting for transfers between devices  50.9 us (17%)
  other arithmetic  19.3 us (6%)
  between operations  14.2 us (5%)
  starting transfers between devices  6.45 us (2%)
    slice x22, matrix products, one_basis(): basis_image = lower_part[:, :, :-1] + upper_part[:, :, 1:]  112 us
    dot_general x11, matrix products, one_basis(): jnp.einsum('ij,vjx->ivx', row_kernel, padded, preferred_element_type=jnp....  39.4 us
    while x66, local copies, waits for them, and re-layouts  29.3 us
    reduce_scatter x1, waiting for transfers between devices, local(): lax.psum_scatter(partial_value[1], 'visit', scatter_dimension=1, tiled=True)  25.3 us
    reduce_scatter x1, waiting for transfers between devices, local(): lax.psum_scatter(partial_value[0], 'visit', scatter_dimension=1, tiled=True)  24.9 us
    squeeze x11, local copies, waits for them, and re-layouts, one_basis(): col_kernel = lax.dynamic_index_in_dim(col_table, which, 0, keepdims=False)  9.34 us
    reduce_sum x1, other arithmetic, batch_terms(): return (jnp.sum(weight * matched, axis=1), jnp.sum(weight, axis=1))  9.03 us
    squeeze x11, local copies, waits for them, and re-layouts, one_basis(): coef_now = lax.dynamic_index_in_dim(coef_block, which, 1, keepdims=False)  7.4 us
  transfers between devices with their start and end apart: 4, of which 2 were waited for; matrix products, arithmetic and copies ran while one was open for 3% of the time, Pallas kernels for 0%

commit v1 on v0

v1 whole, which is shorter than its diff:
```python
import jax
import jax.numpy as jnp
from jax import lax
from jax.experimental import pallas as pl
from jax.experimental.pallas import tpu as pltpu
from jax.sharding import PartitionSpec as P

DITHER = 256
DEPTH_MAX = 16
WIN = 256
PAIR = 2


def row_tables(taps, rows, depth):
    count = taps.shape[1]
    half = count // 2
    spot = jnp.arange(depth, dtype=jnp.int32)
    rel = jnp.where(
        spot < rows,
        spot,
        jnp.where(spot < rows + half, spot - rows - half, spot - half),
    )
    rel = jnp.where(spot < rows + 2 * half, rel, -4 * rows)
    offsets = rel[None, :] - jnp.arange(rows, dtype=jnp.int32)[:, None] + half
    picks = (offsets[None] == jnp.arange(count, dtype=jnp.int32)[:, None, None]).astype(jnp.bfloat16)
    table = jnp.einsum("kt,toi->koi", taps, picks, preferred_element_type=jnp.float32)
    return table.astype(jnp.bfloat16).reshape(-1, depth)


def col_tables(taps, step):
    count = taps.shape[1]
    spot = jnp.arange(WIN, dtype=jnp.int32)
    offsets = jnp.where(spot[None, :] < step, spot[:, None] - spot[None, :], -1)
    picks = (offsets[None] == jnp.arange(count, dtype=jnp.int32)[:, None, None]).astype(jnp.bfloat16)
    table = jnp.einsum("kt,tio->kio", taps, picks, preferred_element_type=jnp.float32)
    return table.astype(jnp.bfloat16)


def coadd_kernel(
    sizes, coef_ref, shift_ref, cover_ref, first_ref, img_ref, inv_ref, row_ref, col_ref,
    num_ref, den_ref, pass_ref,
):
    visits, rows, cols, total_rows, step = sizes
    basis = col_ref.shape[0]
    pairs = img_ref.shape[1] // PAIR
    num_ref[...] = jnp.zeros_like(num_ref)
    den_ref[...] = jnp.zeros_like(den_ref)
    row_ids = first_ref[0] + lax.broadcasted_iota(jnp.int32, (rows, 128), 0)
    row_coord = (2.0 * row_ids.astype(jnp.float32) + 1.0) / total_rows - 1.0
    row_coord = jnp.concatenate([row_coord] * (WIN // 128), axis=1)[None]
    lane = lax.broadcasted_iota(jnp.int32, (PAIR, 1, WIN), 2)
    place = lax.broadcasted_iota(jnp.int32, (PAIR, 1, WIN), 0)

    def one_visit(v, carry):
        @pl.when(cover_ref[v] != 0)
        def _():
            shift = shift_ref[v]

            def one_pair(q, inner):
                col_ids = (q * PAIR + place) * step + lane
                col_coord = (2.0 * col_ids.astype(jnp.float32) + 1.0) / cols - 1.0
                for j in range(PAIR):
                    passed = jnp.dot(
                        row_ref[...], img_ref[v, q * PAIR + j], preferred_element_type=jnp.float32
                    )
                    pass_ref[:, j] = passed.astype(jnp.bfloat16).reshape(basis, rows, WIN)
                matched = jnp.zeros((PAIR, rows, WIN), jnp.float32)
                for k in range(basis):
                    image = jnp.dot(
                        pass_ref[k].reshape(PAIR * rows, WIN),
                        col_ref[k],
                        preferred_element_type=jnp.float32,
                    ).reshape(PAIR, rows, WIN)
                    c0 = coef_ref[v, 3 * k]
                    c1 = coef_ref[v, 3 * k + 1]
                    c2 = coef_ref[v, 3 * k + 2]
                    spatial = (c0 + c1 * col_coord) + c2 * row_coord
                    matched = matched + spatial * image
                inside = (col_ids >= shift) & (col_ids < shift + cols - DITHER)
                where_ok = jnp.broadcast_to(inside, (PAIR, rows, WIN))
                at = pl.ds(q * PAIR, PAIR)
                weight = jnp.where(where_ok, inv_ref[v, at].astype(jnp.float32), 0.0)
                num_ref[at] += weight * matched
                den_ref[at] += weight
                return inner

            lax.fori_loop(0, pairs, one_pair, 0)

        return carry

    lax.fori_loop(0, visits, one_visit, 0)


def local(images, inv_var, row_taps, col_taps, coeffs, dithers, depths):
    visit_count, row_count, col_count = images.shape
    basis, taps = row_taps.shape
    half = taps // 2
    sky = lax.axis_index("sky")
    tiles = lax.axis_size("sky")
    group = lax.axis_index("visit")
    groups = lax.axis_size("visit")
    visits_all = visit_count * groups
    total_rows = row_count * tiles
    step = WIN - 2 * half
    wins = -(-col_count // step)
    wins = -(-wins // PAIR) * PAIR
    depth = -(-(row_count + 2 * half) // 16) * 16

    up = lax.ppermute(
        images[:, row_count - half :], "sky", [(i, i + 1) for i in range(tiles - 1)]
    )
    down = lax.ppermute(images[:, :half], "sky", [(i + 1, i) for i in range(tiles - 1)])
    row_table = row_tables(row_taps, row_count, depth)
    col_table = col_tables(col_taps, step)
    tall = jnp.concatenate([images, up, down], axis=1)
    span = (wins - 1) * step + WIN
    tall = jnp.pad(
        tall,
        ((0, 0), (0, depth - row_count - 2 * half), (half, span - half - col_count)),
    )
    img_win = jnp.stack([tall[:, :, w * step : w * step + WIN] for w in range(wins)], axis=1)
    inv_pad = jnp.pad(inv_var, ((0, 0), (0, 0), (0, span - col_count)))
    inv_win = jnp.stack([inv_pad[:, :, w * step : w * step + WIN] for w in range(wins)], axis=1)

    order = group * visit_count + jnp.arange(visit_count, dtype=jnp.int32)
    first_visit = sky * visits_all // tiles
    covered = (jnp.mod(order - first_visit, visits_all) < depths[0]).astype(jnp.int32)
    coef = lax.dynamic_slice_in_dim(coeffs, group * visit_count, visit_count, 0)
    coef = coef.reshape(visit_count, basis * 3)
    shifts = lax.dynamic_slice_in_dim(dithers, group * visit_count, visit_count, 0)
    first_row = (sky * row_count).astype(jnp.int32).reshape(1)

    smem = pl.BlockSpec(memory_space=pltpu.SMEM)
    vmem = pl.BlockSpec(memory_space=pltpu.VMEM)
    out = jax.ShapeDtypeStruct((wins, row_count, WIN), jnp.float32)
    sizes = (visit_count, row_count, col_count, total_rows, step)

    def body(*refs):
        coadd_kernel(sizes, *refs)

    num, den = pl.pallas_call(
        body,
        out_shape=(out, out),
        in_specs=[smem] * 4 + [vmem] * 4,
        out_specs=(vmem, vmem),
        scratch_shapes=[pltpu.VMEM((basis, PAIR, row_count, WIN), jnp.bfloat16)],
        compiler_params=pltpu.CompilerParams(vmem_limit_bytes=48 * 1024 * 1024),
    )(coef, shifts, covered, first_row, img_win, inv_win, row_table, col_table)

    def flat(x):
        return jnp.concatenate([x[w, :, :step] for w in range(wins)], axis=1)[:, :col_count]

    both = jnp.stack([flat(num), flat(den)], axis=0)
    both = lax.psum_scatter(both, "visit", scatter_dimension=2, tiled=True)
    return both[0] / (1.0 + both[1])


def solution(mesh):
    placed = (P("visit", "sky", None), P("visit", "sky", None), P(), P(), P(), P(), P("sky"))
    return jax.shard_map(
        local, mesh=mesh, in_specs=placed, out_specs=P("sky", "visit"), check_vma=False
    )
```

time: 306 us -> 131 us (0.43)
  matrix products: 154 us -> 4.73 us
  local copies, waits for them, and re-layouts: 57.5 us -> 25 us
  Pallas kernels: 0 us -> 12.7 us
  other arithmetic: 19.3 us -> 6.96 us
  waiting for transfers between devices: 50.9 us -> 60.8 us
    slice x22 -> x0, matrix products: 112 us -> none  [one_basis(): basis_image = lower_part[:, :, :-1] + upper_part[:, :, 1:]]
    dot_general x13 -> x2, matrix products: 42.3 us -> 4.73 us  [the longest x1 3.95 us: col_tables(): jnp.einsum('kt,tio->kio', taps, picks, preferred_element_type=jnp.float32)]
    while x66 -> x0, local copies, waits for them, and re-layouts: 29.3 us -> none
    squeeze x22 -> x2, local copies, waits for them, and re-layouts: 16.7 us -> 0.14 us  [flat(): x[w, :, :step]]
    pallas_call x0 -> x1, Pallas kernels: none -> 12.7 us  [local(): pl.pallas_call(body, out_shape=(out, out), in_specs=[smem] * 4 + [vmem] *...]
    unnamed x12 -> x36, local copies, waits for them, and re-layouts: 3.65 us -> 14.4 us
    reduce_scatter x2 -> x1, waiting for transfers between devices: 50.2 us -> 60.8 us  [local(): both = lax.psum_scatter(both, 'visit', scatter_dimension=2, tiled=True)]
    reduce_sum x1 -> x0, other arithmetic: 9.03 us -> none  [batch_terms(): return (jnp.sum(weight * matched, axis=1), jnp.sum(weight, axis=1))]
  transfers between devices with their start and end apart: 4 -> 3, of which waited for: 2 -> 1; matrix products, arithmetic and copies ran while one was open for 3% -> 13% of each run, Pallas kernels for 0% -> 0%
where the time goes in v1:
time: 131 us
  waiting for transfers between devices  60.8 us (46%)
  local copies, waits for them, and re-layouts  25 us (19%)
  between operations  14.4 us (11%)
  Pallas kernels  12.7 us (10%)
  other arithmetic  6.96 us (5%)
  starting transfers between devices  6.54 us (5%)
  matrix products  4.73 us (4%)
    reduce_scatter x1, waiting for transfers between devices, local(): both = lax.psum_scatter(both, 'visit', scatter_dimension=2, tiled=True)  60.8 us
    unnamed x36, local copies, waits for them, and re-layouts  14.4 us
    pallas_call x1, Pallas kernels, local(): pl.pallas_call(body, out_shape=(out, out), in_specs=[smem] * 4 + [vmem] *...  12.7 us
    ppermute x1, starting transfers between devices, local(): lax.ppermute(images[:, row_count - half:], 'sky', [(i, i + 1) for i in ra...  4.5 us
    dot_general x1, matrix products, col_tables(): jnp.einsum('kt,tio->kio', taps, picks, preferred_element_type=jnp.float32)  3.95 us
    concatenate x1, other arithmetic, local(): tall = jnp.concatenate([images, up, down], axis=1)  3.83 us
  transfers between devices with their start and end apart: 3, of which 1 were waited for; matrix products, arithmetic and copies ran while one was open for 13% of the time, Pallas kernels for 0%

profile of v1, /device:TPU:1, one launch (start us, length us, event | category | flops | bytes accessed | tf_op | source)
XLA Modules:
  0.0 131.1 jit_solution(7645966919175173683)
XLA Ops:
  6.5 1.8 %fusion.36 = (bf16[8,20,2048]{2,1,0:T(8,128)(2,1)S(1)}, bf16[8,20,2048]{2,1,0:T(8,128)(2,1)S(1)}) fusion(bf16[8,96,2048]{2,1,0:T(8,128)(2,1)} %param.7), kind=kLoop, calls=%fused_computation.99 | loop fusion | bytes 2621440 | tf_op jit(solution)/shard_map/slice | solution.py:110
  8.3 1.2 copy.48
  9.5 4.5 %collective-permute-start = (bf16[8,20,2048]{2,0,1:T(8,128)(2,1)}, bf16[8,20,2048]{2,0,1:T(8,128)(2,1)}, u32[]{:S(2)}, u32[]{:S(2)}) collective-permute-start(bf16[8,20,2048]{2,0,1:T(8,128)(2,1)} %copy.48), channel_id=1, source_target_pairs={{0,4},{4,8},{8,12},{12,16},{16,20},{20,24},{24,28},{1,5},{5,9},{9,... | collective-permute-start | bytes 1966088 | tf_op jit(solution)/shard_map/ppermute | solution.py:109
  14.0 1.2 copy.49
  15.2 2.0 %collective-permute-start.1 = (bf16[8,20,2048]{2,0,1:T(8,128)(2,1)}, bf16[8,20,2048]{2,0,1:T(8,128)(2,1)}, u32[]{:S(2)}, u32[]{:S(2)}) collective-permute-start(bf16[8,20,2048]{2,0,1:T(8,128)(2,1)} %copy.49), channel_id=1, source_target_pairs={{4,0},{8,4},{12,8},{16,12},{20,16},{24,20},{28,24},{5,1},{9,5},{13... | collective-permute-start | bytes 1966088 | tf_op jit(solution)/shard_map/ppermute | solution.py:112
  19.2 1.9 %copy-done.4 = bf16[8,10,96,256]{3,2,1,0:T(8,128)(2,1)} copy-done((bf16[8,10,96,256]{3,2,1,0:T(8,128)(2,1)}, bf16[8,10,96,256]{3,2,1,0:T(8,128)(2,1)S(1)}, u32[]{:S(2)}) %copy-start.4) | copy-done | bytes 3932184
  21.4 4.0 %fusion = bf16[256,256,11]{1,2,0:T(8,128)(2,1)} fusion(s32[256,256]{1,0:T(8,128)S(1)} %subtract_select_fusion, bf16[11,41]{1,0:T(8,128)(2,1)S(1)} %copy-done.5), kind=kOutput, calls=%fused_computation.3 | convolution fusion | flops 61800448 | bytes 1704838 | tf_op jit(solution)/shard_map/kt,tio->kio/dot_general | solution.py:35
  25.3 0.8 fusion.16
  26.3 2.1 %copy.53 = bf16[256,256,11]{1,0,2:T(8,128)(2,1)S(1)} copy(bf16[256,256,11]{1,2,0:T(8,128)(2,1)} %fusion) | data formatting | bytes 2883584 | tf_op jit(solution)/shard_map/kt,tio->kio/dot_general | solution.py:35
  28.4 0.4 copy.45
  28.9 2.2 %bitcast_dynamic-update-slice_fusion.1 = bf16[8,10,96,256]{3,2,1,0:T(8,128)(2,1)} fusion(bf16[8,10,96,256]{3,2,1,0:T(8,128)(2,1)} %copy-done.4, bf16[8,96,2048]{2,1,0:T(8,128)(2,1)} %param.8), kind=kLoop, calls=%fused_computation.50 | loop fusion | bytes 786432
  31.0 2.0 %bitcast_dynamic-update-slice_fusion = bf16[8,10,96,256]{3,2,1,0:T(8,128)(2,1)} fusion(bf16[8,10,96,256]{3,2,1,0:T(8,128)(2,1)} %bitcast_dynamic-update-slice_fusion.1, bf16[8,96,2048]{2,1,0:T(8,128)(2,1)} %param.8), kind=kLoop, calls=%fused_computation.49 | loop fusion | bytes 786432
  33.1 1.8 %fusion.28.refs_5_ = bf16[8,10,96,256]{3,2,1,0:T(8,128)(2,1)} fusion(bf16[8,10,96,256]{3,2,1,0:T(8,128)(2,1)} %bitcast_dynamic-update-slice_fusion, bf16[8,96,2048]{2,1,0:T(8,128)(2,1)} %param.8), kind=kLoop, calls=%fused_computation.48 | loop fusion | bytes 3538944 | tf_op jit(solution)/shard_map/stack | solution.py:123
  34.9 1.5 %copy.34 = bf16[8,20,2048]{2,1,0:T(8,128)(2,1)S(1)} copy(bf16[8,20,2048]{2,0,1:T(8,128)(2,1)} %collective-permute-done) | data formatting | bytes 1310720 | tf_op jit(solution)/shard_map/ppermute | solution.py:109
  36.4 1.5 %copy.35 = bf16[8,20,2048]{2,1,0:T(8,128)(2,1)S(1)} copy(bf16[8,20,2048]{2,0,1:T(8,128)(2,1)} %collective-permute-done.1) | data formatting | bytes 1310720 | tf_op jit(solution)/shard_map/ppermute | solution.py:112
  37.9 3.8 %fusion.9 = bf16[8,144,2200]{2,1,0:T(8,128)(2,1)S(1)} fusion(bf16[8,20,2048]{2,1,0:T(8,128)(2,1)S(1)} %copy.35, bf16[8,20,2048]{2,1,0:T(8,128)(2,1)S(1)} %copy.34, bf16[8,96,2048]{2,1,0:T(8,128)(2,1)S(1)} %copy-done.3), kind=kLoop, calls=%fused_computation.13 | loop fusion | flops 43084800 | bytes 9525248 | tf_op jit(solution)/shard_map/concatenate | solution.py:115
  41.8 0.3 fusion.25
  42.0 0.3 fusion.24
  42.3 0.3 fusion.23
  42.6 0.3 fusion.22
  42.8 0.3 fusion.21
  43.1 0.3 fusion.20
  43.4 0.3 fusion.19
  43.6 0.3 fusion.18
  43.9 0.3 fusion.17.refs_4_
  44.2 2.5 %copy-done.2 = bf16[8,10,144,256]{3,2,1,0:T(8,128)(2,1)} copy-done((bf16[8,10,144,256]{3,2,1,0:T(8,128)(2,1)}, bf16[8,10,144,256]{3,2,1,0:T(8,128)(2,1)S(1)}, u32[]{:S(2)}) %copy-start.2) | copy-done | bytes 5898264
  46.7 12.7 %shard_map.73 = (f32[10,96,256]{2,1,0:T(8,128)S(1)}, f32[10,96,256]{2,1,0:T(8,128)S(1)}) custom-call(f32[8,33]{1,0:T(8,128)S(1)} %copy.47.refs_0_, s32[8]{0:T(128)S(1)} %dynamic_slice.7.refs_1_, s32[8]{0:T(128)S(1)} %compare_convert_fusion.refs_2_, s32[1]{0:T(128)} %bitcast.1.refs_3_, bf16[8,10,144,256]{3,2,1,0:T(8,128)(2,1)} %copy-done.2, ...), custom_call_target="tpu_custom_call" | custom-call | tf_op jit(solution)/shard_map/pallas_call | solution.py:141
  59.5 0.4 concatenate.10
  59.9 0.4 concatenate.11
  60.4 1.3 pad_maximum_fusion
  61.7 60.8 %reduce-scatter.2.cloned.1.call-done = f32[2,96,512]{2,1,0:T(8,128)} async-done(((f32[2,96,2048]{2,1,0:T(8,128)}), f32[2,96,512]{2,1,0:T(8,128)}) %reduce-scatter.2.cloned.1.call-update) | async-done | bytes 393232 | tf_op jit(solution)/shard_map/reduce_scatter | solution.py:154
  122.5 1.7 %fusion.30 = f32[96,512]{1,0:T(8,128)} fusion(f32[2,96,512]{2,1,0:T(8,128)} %reduce-scatter.2.cloned.1.call-done), kind=kLoop, calls=%fused_computation.61 | loop fusion | flops 98304 | bytes 589824 | tf_op jit(solution)/shard_map/div | solution.py:155
  (38 shorter events, 2.0 us)
Async XLA Ops:
  6.5 14.8 %copy-start = (f32[32,11,3]{0,2,1:T(4,128)S(1)}, f32[32,11,3]{0,2,1:T(4,128)}, u32[]{:S(2)}) copy-start(f32[32,11,3]{0,2,1:T(4,128)} %param.11) | copy-start | bytes 12676
  6.5 11.4 %copy-start.1 = (bf16[8,96,2048]{2,1,0:T(8,128)(2,1)S(1)}, bf16[8,96,2048]{2,1,0:T(8,128)(2,1)}, u32[]{:S(2)}) copy-start(bf16[8,96,2048]{2,1,0:T(8,128)(2,1)} %param.8) | copy-start | bytes 9437188
  6.5 14.8 %copy-start.5 = (bf16[11,41]{1,0:T(8,128)(2,1)S(1)}, bf16[11,41]{1,0:T(8,128)(2,1)}, u32[]{:S(2)}) copy-start(bf16[11,41]{1,0:T(8,128)(2,1)} %param.10) | copy-start | bytes 2710
  6.5 116.0 %reduce-scatter.2.cloned.1.call-start = ((), (), s32[]{:S(2)}) async-start(), calls=%async_computation.1 | async-start | bytes 1966080 | tf_op jit(solution)/shard_map/reduce_scatter | solution.py:154
  9.5 25.4 %collective-permute-start = (bf16[8,20,2048]{2,0,1:T(8,128)(2,1)}, bf16[8,20,2048]{2,0,1:T(8,128)(2,1)}, u32[]{:S(2)}, u32[]{:S(2)}) collective-permute-start(bf16[8,20,2048]{2,0,1:T(8,128)(2,1)} %copy.48), channel_id=1, source_target_pairs={{0,4},{4,8},{8,12},{12,16},{16,20},{20,24},{24,28},{1,5},{5,9},{9,... | collective-permute-start | bytes 1966088 | tf_op jit(solution)/shard_map/ppermute | solution.py:109
  14.0 11.3 %copy-start.6 = (bf16[11,41]{1,0:T(8,128)(2,1)S(1)}, bf16[11,41]{1,0:T(8,128)(2,1)}, u32[]{:S(2)}) copy-start(bf16[11,41]{1,0:T(8,128)(2,1)} %param.9) | copy-start | bytes 2710
  15.2 11.0 %copy-start.7 = (s32[32]{0:T(128)S(1)}, s32[32]{0:T(128)}, u32[]{:S(2)}) copy-start(s32[32]{0:T(128)} %param.12) | copy-start | bytes 388
  15.2 21.2 %collective-permute-start.1 = (bf16[8,20,2048]{2,0,1:T(8,128)(2,1)}, bf16[8,20,2048]{2,0,1:T(8,128)(2,1)}, u32[]{:S(2)}, u32[]{:S(2)}) collective-permute-start(bf16[8,20,2048]{2,0,1:T(8,128)(2,1)} %copy.49), channel_id=1, source_target_pairs={{4,0},{8,4},{12,8},{16,12},{20,16},{24,20},{28,24},{5,1},{9,5},{13... | collective-permute-start | bytes 1966088 | tf_op jit(solution)/shard_map/ppermute | solution.py:112
  19.2 1.9 %copy-start.4 = (bf16[8,10,96,256]{3,2,1,0:T(8,128)(2,1)}, bf16[8,10,96,256]{3,2,1,0:T(8,128)(2,1)S(1)}, u32[]{:S(2)}) copy-start(bf16[8,10,96,256]{3,2,1,0:T(8,128)(2,1)S(1)} %bitcast_dynamic-update-slice_fusion.2) | copy-start | bytes 11796484
  28.9 9.0 %copy-start.3 = (bf16[8,96,2048]{2,1,0:T(8,128)(2,1)S(1)}, bf16[8,96,2048]{2,1,0:T(8,128)(2,1)}, u32[]{:S(2)}) copy-start(bf16[8,96,2048]{2,1,0:T(8,128)(2,1)} %param.7) | copy-start | bytes 9437188
  44.2 2.5 %copy-start.2 = (bf16[8,10,144,256]{3,2,1,0:T(8,128)(2,1)}, bf16[8,10,144,256]{3,2,1,0:T(8,128)(2,1)S(1)}, u32[]{:S(2)}) copy-start(bf16[8,10,144,256]{3,2,1,0:T(8,128)(2,1)S(1)} %fusion.17.refs_4_) | copy-start | bytes 17694724
Sparse Core Ops, SparseCore 0:
  61.9 60.6 reduce-scatter.1

commit v2 on v1

v2 whole, which is shorter than its diff:
```python
import jax
import jax.numpy as jnp
from jax import lax
from jax.experimental import pallas as pl
from jax.experimental.pallas import tpu as pltpu
from jax.sharding import PartitionSpec as P

DITHER = 256
DEPTH_MAX = 16
WIN = 256
PAIR = 2
LANE = 128
EDGE = 32
MESH = pl.DeviceIdType.MESH


def base_rows(row_taps, col_taps, rows):
    basis, taps = row_taps.shape
    half = taps // 2
    spot = jnp.arange(WIN, dtype=jnp.int32)

    def placed(table, which):
        picks = which[None, :] == jnp.arange(taps, dtype=jnp.int32)[:, None]
        return jnp.sum(
            jnp.where(picks[None], table.astype(jnp.float32)[:, :, None], 0.0), axis=1
        )

    own = placed(row_taps, jnp.mod(spot + half, WIN))
    above = placed(row_taps, spot - (LANE + EDGE - half))
    across = placed(col_taps, jnp.mod(-spot, WIN))
    return jnp.stack([own, above, across], axis=1)


def kernel(
    sizes,
    coef_ref, shift_ref, depth_ref, base_ref, img_ref, inv_ref,
    out_ref,
    buf, inv, row_tab, col_tab, passed, acc, flat, outgo, income,
    img_sem, inv_sem, halo_send, halo_recv, part_send, part_recv,
):
    tiles, groups, step = sizes
    visits, rows, cols = img_ref.shape
    basis = base_ref.shape[0]
    visits_all = visits * groups
    total_rows = rows * tiles
    strip = cols // groups
    width = buf.shape[2]
    deep = rows + 2 * EDGE
    pairs = groups + 1
    body = pl.ds(LANE, cols)

    t = lax.axis_index("sky")
    g = lax.axis_index("visit")
    first = lax.div(t * visits_all, tiles)

    def needs(tile, v):
        start = lax.div(tile * visits_all, tiles)
        return lax.rem(g * visits + v - start + visits_all, visits_all) < DEPTH_MAX

    def gives(group):
        o = lax.rem(group - lax.div(first, visits) + groups, groups)
        return (o * visits - lax.rem(first, visits)) < DEPTH_MAX

    barrier = pltpu.get_barrier_semaphore()

    @pl.when(t > 0)
    def _():
        pl.semaphore_signal(barrier, inc=1, device_id=(t - 1, g), device_id_type=MESH)

    @pl.when(t < tiles - 1)
    def _():
        pl.semaphore_signal(barrier, inc=1, device_id=(t + 1, g), device_id_type=MESH)

    for d in range(1, groups):
        pl.semaphore_signal(
            barrier, inc=1, device_id=(t, lax.rem(g + d, groups)), device_id_type=MESH
        )

    def img_copy(v):
        return pltpu.make_async_copy(
            img_ref.at[v], buf.at[v, pl.ds(0, rows), body], img_sem.at[v]
        )

    def inv_copy(v):
        return pltpu.make_async_copy(
            inv_ref.at[v], inv.at[v, :, pl.ds(0, cols)], inv_sem.at[v]
        )

    def start_local(v, carry):
        @pl.when(needs(t, v))
        def _():
            img_copy(v).start()
            inv_copy(v).start()

        return carry

    lax.fori_loop(0, visits, start_local, 0)

    def clear(v, carry):
        buf[v, :, :LANE] = jnp.zeros((deep, LANE), jnp.bfloat16)
        buf[v, :, LANE + cols :] = jnp.zeros((deep, width - LANE - cols), jnp.bfloat16)
        inv[v, :, cols:] = jnp.zeros((rows, inv.shape[2] - cols), jnp.bfloat16)

        @pl.when(t == 0)
        def _():
            buf[v, rows + EDGE :, LANE : LANE + cols] = jnp.zeros((EDGE, cols), jnp.bfloat16)

        @pl.when(t == tiles - 1)
        def _():
            buf[v, rows : rows + EDGE, LANE : LANE + cols] = jnp.zeros((EDGE, cols), jnp.bfloat16)

        return carry

    lax.fori_loop(0, visits, clear, 0)

    lower = jnp.where(t > 0, 1, 0)
    upper = jnp.where(t < tiles - 1, 1, 0)
    pl.semaphore_wait(barrier, groups - 1 + lower + upper)

    def to_next(v):
        return pltpu.make_async_remote_copy(
            src_ref=img_ref.at[v, pl.ds(rows - EDGE, EDGE)],
            dst_ref=buf.at[v, pl.ds(rows + EDGE, EDGE), body],
            send_sem=halo_send.at[0, v],
            recv_sem=halo_recv.at[0, v],
            device_id=(lax.rem(t + 1, tiles), g),
            device_id_type=MESH,
        )

    def to_last(v):
        return pltpu.make_async_remote_copy(
            src_ref=img_ref.at[v, pl.ds(0, EDGE)],
            dst_ref=buf.at[v, pl.ds(rows, EDGE), body],
            send_sem=halo_send.at[1, v],
            recv_sem=halo_recv.at[1, v],
            device_id=(lax.rem(t + tiles - 1, tiles), g),
            device_id_type=MESH,
        )

    def sends(v, act):
        @pl.when((t < tiles - 1) & needs(t + 1, v))
        def _():
            act(to_next(v))

        @pl.when((t > 0) & needs(t - 1, v))
        def _():
            act(to_last(v))

    def start_halo(v, carry):
        sends(v, lambda c: c.start())
        return carry

    lax.fori_loop(0, visits, start_halo, 0)

    def one_table(k, carry):
        def spread(which, count):
            line = jnp.broadcast_to(base_ref[k, pl.ds(which, 1), :], (count, WIN))
            return pltpu.roll(line, 0, 1, stride=1, stride_axis=0)

        own = spread(0, rows)[:, :LANE]
        above = spread(1, rows)[:, LANE:]
        both = jnp.concatenate([own, above], axis=1).astype(jnp.bfloat16)
        row_tab[k] = both[:, :deep]
        col_tab[k] = spread(2, WIN).astype(jnp.bfloat16)
        return carry

    lax.fori_loop(0, basis, one_table, 0)
    flat[...] = jnp.zeros_like(flat)

    row_ids = t * rows + lax.broadcasted_iota(jnp.int32, (rows, LANE), 0)
    row_coord = (2.0 * row_ids.astype(jnp.float32) + 1.0) / total_rows - 1.0
    row_coord = jnp.concatenate([row_coord] * (WIN // LANE), axis=1)[None]
    lane = lax.broadcasted_iota(jnp.int32, (PAIR, 1, WIN), 2)
    place = lax.broadcasted_iota(jnp.int32, (PAIR, 1, WIN), 0)

    def window(ref, v, at):
        base = pl.multiple_of(lax.div(at, LANE) * LANE, LANE)
        chunk = ref[v, :, pl.ds(base, WIN + LANE)].astype(jnp.float32)
        turn = lax.rem(WIN + LANE - lax.rem(at, LANE), WIN + LANE)
        return pltpu.roll(chunk, turn, 1)[:, :WIN]

    ascend = g >= groups // 2

    def one_pair(s, carry):
        q = jnp.where(ascend, s, pairs - 1 - s)
        acc[...] = jnp.zeros_like(acc)
        col_ids = (q * PAIR + place) * step + lane
        col_coord = (2.0 * col_ids.astype(jnp.float32) + 1.0) / cols - 1.0

        def one_visit(v, inner):
            @pl.when(needs(t, v))
            def _():
                @pl.when(s == 0)
                def _():
                    img_copy(v).wait()
                    inv_copy(v).wait()

                    @pl.when(t > 0)
                    def _():
                        to_next(v).wait_recv()

                    @pl.when(t < tiles - 1)
                    def _():
                        to_last(v).wait_recv()

                who = g * visits + v
                shift = shift_ref[who]
                on = lax.rem(who - first + visits_all, visits_all) < depth_ref[0]
                scale = jnp.where(on, 1.0, 0.0)
                weights = []
                for j in range(PAIR):
                    at = (q * PAIR + j) * step
                    tall = window(buf, v, at + LANE - (WIN - step) // 2)
                    made = jnp.dot(
                        row_tab[...].reshape(basis * rows, deep),
                        tall.astype(jnp.bfloat16),
                        preferred_element_type=jnp.float32,
                    )
                    passed[:, j] = made.astype(jnp.bfloat16).reshape(basis, rows, WIN)
                    weights.append(window(inv, v, at))
                matched = jnp.zeros((PAIR, rows, WIN), jnp.float32)
                for k in range(basis):
                    image = jnp.dot(
                        passed[k].reshape(PAIR * rows, WIN),
                        col_tab[k],
                        preferred_element_type=jnp.float32,
                    ).reshape(PAIR, rows, WIN)
                    c0 = coef_ref[(who * basis + k) * 3]
                    c1 = coef_ref[(who * basis + k) * 3 + 1]
                    c2 = coef_ref[(who * basis + k) * 3 + 2]
                    matched = matched + ((c0 + c1 * col_coord) + c2 * row_coord) * image
                inside = (col_ids >= shift) & (col_ids < shift + cols - DITHER) & (lane < step)
                weight = jnp.stack(weights) * jnp.where(inside, scale, 0.0)
                acc[0] += weight * matched
                acc[1] += weight

            return inner

        lax.fori_loop(0, visits, one_visit, 0)

        @pl.when(gives(g))
        def _():
            for j in range(PAIR):
                at = (q * PAIR + j) * step
                base = pl.multiple_of(lax.div(at, LANE) * LANE, LANE)
                for n in range(2):
                    part = acc[n, j]
                    part = jnp.concatenate([part, jnp.zeros((rows, LANE), jnp.float32)], axis=1)
                    flat[n, :, pl.ds(base, WIN + LANE)] += pltpu.roll(part, lax.rem(at, LANE), 1)

            c = jnp.where(ascend, s - 1, pairs - 1 - s)

            @pl.when((s > 0) & (c != g))
            def _():
                d = lax.rem(c - g + groups, groups)
                for n in range(2):
                    here = flat[n, :, pl.ds(pl.multiple_of(c * strip, LANE), strip)]
                    outgo[d - 1, n] = here.astype(jnp.bfloat16)
                part_copy(d).start()

        return carry

    def part_copy(d):
        return pltpu.make_async_remote_copy(
            src_ref=outgo.at[d - 1],
            dst_ref=income.at[d - 1],
            send_sem=part_send.at[d - 1],
            recv_sem=part_recv.at[d - 1],
            device_id=(t, lax.rem(g + d, groups)),
            device_id_type=MESH,
        )

    lax.fori_loop(0, pairs, one_pair, 0)

    mine = pl.ds(pl.multiple_of(g * strip, LANE), strip)
    for d in range(1, groups):
        @pl.when(gives(lax.rem(g - d + groups, groups)))
        def _():
            part_copy(d).wait_recv()
            for n in range(2):
                flat[n, :, mine] += income[d - 1, n].astype(jnp.float32)

    out_ref[...] = flat[0, :, mine] / (1.0 + flat[1, :, mine])

    @pl.when(gives(g))
    def _():
        for d in range(1, groups):
            part_copy(d).wait_send()

    def end_halo(v, carry):
        sends(v, lambda c: c.wait_send())
        return carry

    lax.fori_loop(0, visits, end_halo, 0)


def local(images, inv_var, row_taps, col_taps, coeffs, dithers, depths):
    visits, rows, cols = images.shape
    basis, taps = row_taps.shape
    tiles = lax.axis_size("sky")
    groups = lax.axis_size("visit")
    step = WIN - taps + 1
    pairs = groups + 1
    strip = cols // groups
    room = cols + WIN
    deep = rows + 2 * EDGE
    bases = base_rows(row_taps, col_taps, rows)
    sizes = (tiles, groups, step)

    def run(*refs):
        kernel(sizes, *refs)

    smem = pl.BlockSpec(memory_space=pltpu.SMEM)
    vmem = pl.BlockSpec(memory_space=pltpu.VMEM)
    hbm = pl.BlockSpec(memory_space=pl.ANY)
    dma = pltpu.SemaphoreType.DMA
    flops = 2 * visits * pairs * PAIR * 2 * basis * rows * WIN * WIN
    return pl.pallas_call(
        run,
        out_shape=jax.ShapeDtypeStruct((rows, strip), jnp.float32),
        in_specs=[smem, smem, smem, vmem, hbm, hbm],
        out_specs=vmem,
        scratch_shapes=[
            pltpu.VMEM((visits, deep, LANE + cols + WIN), jnp.bfloat16),
            pltpu.VMEM((visits, rows, room), jnp.bfloat16),
            pltpu.VMEM((basis, rows, deep), jnp.bfloat16),
            pltpu.VMEM((basis, WIN, WIN), jnp.bfloat16),
            pltpu.VMEM((basis, PAIR, rows, WIN), jnp.bfloat16),
            pltpu.VMEM((2, PAIR, rows, WIN), jnp.float32),
            pltpu.VMEM((2, rows, room), jnp.float32),
            pltpu.VMEM((groups - 1, 2, rows, strip), jnp.bfloat16),
            pltpu.VMEM((groups - 1, 2, rows, strip), jnp.bfloat16),
            dma((visits,)),
            dma((visits,)),
            dma((2, visits)),
            dma((2, visits)),
            dma((groups - 1,)),
            dma((groups - 1,)),
        ],
        compiler_params=pltpu.CompilerParams(
            vmem_limit_bytes=48 * 1024 * 1024, collective_id=0, has_side_effects=True
        ),
        cost_estimate=pl.CostEstimate(
            flops=flops, bytes_accessed=4 * visits * rows * cols, transcendentals=0
        ),
    )(coeffs.reshape(-1), dithers, depths, bases, images, inv_var)


def solution(mesh):
    placed = (P("visit", "sky", None), P("visit", "sky", None), P(), P(), P(), P(), P("sky"))
    return jax.shard_map(
        local, mesh=mesh, in_specs=placed, out_specs=P("sky", "visit"), check_vma=False
    )
```

time: 131 us -> 67.4 us (0.51)
  the two profiles are of different devices: /device:TPU:1 before, /device:TPU:28 now
where the time goes in v2:
time: 67.4 us; the launch traced here: 67.1 us
  Pallas kernels  60.1 us (89%)
  local copies, waits for them, and re-layouts  4.36 us (6%)
  other arithmetic  1.82 us (3%)
  between operations  0.76 us (1%)
    pallas_call x1, Pallas kernels, local(): pl.pallas_call(run, out_shape=jax.ShapeDtypeStruct((rows, strip), jnp.flo...  60.1 us
    unnamed x6, local copies, waits for them, and re-layouts  4.14 us
    convert_element_type x2, other arithmetic, placed(): table.astype(jnp.float32)[:, :, None]  1.38 us

profile of v2, /device:TPU:28, one launch (start us, length us, event | category | flops | bytes accessed | tf_op | source)
XLA Modules:
  0.0 67.1 jit_solution(7426960212075892389)
XLA Ops:
  0.7 0.7 %convert_element_type.7 = f32[11,41]{1,0:T(8,128)S(1)} convert(bf16[11,41]{1,0:T(8,128)(2,1)} %param.9) | non-fusion elementwise | flops 451 | bytes 2706 | tf_op jit(solution)/shard_map/convert_element_type | solution.py:25
  1.4 0.7 %convert_element_type.8 = f32[11,41]{1,0:T(8,128)S(1)} convert(bf16[11,41]{1,0:T(8,128)(2,1)} %param.10) | non-fusion elementwise | flops 451 | bytes 2706 | tf_op jit(solution)/shard_map/convert_element_type | solution.py:25
  2.1 0.2 select_reduce_fusion
  2.3 0.2 select_reduce_fusion.2
  2.6 0.9 %copy.9 = f32[32,11,3]{2,1,0:T(8,128)S(1)} copy(f32[32,11,3]{0,2,1:T(4,128)} %param.11) | data formatting | bytes 8448 | tf_op args[4]
  3.5 0.2 reshape.99.refs_0_
  3.7 0.0 copy-start
  3.7 1.9 %copy-done = bf16[8,96,2048]{2,1,0:T(8,128)(2,1)S(1)} copy-done((bf16[8,96,2048]{2,1,0:T(8,128)(2,1)S(1)}, bf16[8,96,2048]{2,1,0:T(8,128)(2,1)}, u32[]{:S(2)}) %copy-start) | copy-done | bytes 3145752
  5.6 0.0 copy-start.1
  5.6 0.7 copy-done.1
  6.2 60.1 %shard_map.73 = f32[96,512]{1,0:T(8,128)S(1)} custom-call(f32[1056]{0:T(1024)S(1)} %reshape.99.refs_0_, s32[32]{0:T(128)S(1)} %copy-done.1, s32[1]{0:T(128)S(6)} %copy.11.refs_2_, f32[11,3,256]{2,1,0:T(4,128)S(1)} %pad_maximum_fusion.refs_3_, bf16[8,96,2048]{2,1,0:T(8,128)(2,1)S(1)} %copy-done, bf16[8,96,2048]{2,1,0:T(8,128)(2,1)} %refs_5_.1), custom_call_target="tpu_custom_call" | custom-call | flops 22145925120 | bytes 6291456 | tf_op jit(solution)/shard_map/pallas_call | solution.py:318
  66.4 0.7 %copy.12 = f32[96,512]{1,0:T(8,128)} copy(f32[96,512]{1,0:T(8,128)S(1)} %shard_map.73) | data formatting | bytes 393216
  (9 shorter events, 0.1 us)
Async XLA Ops:
  3.7 1.9 %copy-start = (bf16[8,96,2048]{2,1,0:T(8,128)(2,1)S(1)}, bf16[8,96,2048]{2,1,0:T(8,128)(2,1)}, u32[]{:S(2)}) copy-start(bf16[8,96,2048]{2,1,0:T(8,128)(2,1)} %refs_4_.1) | copy-start | bytes 9437188
  5.6 0.7 copy-start.1

commit v3 on v2

--- a/solution.py
+++ b/solution.py
@@ -14,33 +14,17 @@
 MESH = pl.DeviceIdType.MESH
 
 
-def base_rows(row_taps, col_taps, rows):
-    basis, taps = row_taps.shape
-    half = taps // 2
-    spot = jnp.arange(WIN, dtype=jnp.int32)
-
-    def placed(table, which):
-        picks = which[None, :] == jnp.arange(taps, dtype=jnp.int32)[:, None]
-        return jnp.sum(
-            jnp.where(picks[None], table.astype(jnp.float32)[:, :, None], 0.0), axis=1
-        )
-
-    own = placed(row_taps, jnp.mod(spot + half, WIN))
-    above = placed(row_taps, spot - (LANE + EDGE - half))
-    across = placed(col_taps, jnp.mod(-spot, WIN))
-    return jnp.stack([own, above, across], axis=1)
-
-
 def kernel(
     sizes,
-    coef_ref, shift_ref, depth_ref, base_ref, img_ref, inv_ref,
+    coef_ref, shift_ref, depth_ref, row_ref, col_ref, img_ref, inv_ref,
     out_ref,
-    buf, inv, row_tab, col_tab, passed, acc, flat, outgo, income,
+    buf, inv, base_ref, row_tab, col_tab, pass_a, pass_b, acc, flat, outgo, income,
     img_sem, inv_sem, halo_send, halo_recv, part_send, part_recv,
 ):
     tiles, groups, step = sizes
     visits, rows, cols = img_ref.shape
-    basis = base_ref.shape[0]
+    basis, taps = row_ref.shape
+    half = taps // 2
     visits_all = visits * groups
     total_rows = rows * tiles
     strip = cols // groups
@@ -57,6 +41,13 @@
         start = lax.div(tile * visits_all, tiles)
         return lax.rem(g * visits + v - start + visits_all, visits_all) < DEPTH_MAX
 
+    turn = lax.rem(g - lax.div(first, visits) + groups, groups)
+    part = lax.rem(first, visits)
+    lo = jnp.where(turn == 0, part, 0)
+    hi = jnp.clip(DEPTH_MAX + part - turn * visits, 0, visits)
+    twos = lax.div(jnp.maximum(hi - lo, 0) + 1, 2)
+    ascend = g >= groups // 2
+
     def gives(group):
         o = lax.rem(group - lax.div(first, visits) + groups, groups)
         return (o * visits - lax.rem(first, visits)) < DEPTH_MAX
@@ -117,44 +108,75 @@
     upper = jnp.where(t < tiles - 1, 1, 0)
     pl.semaphore_wait(barrier, groups - 1 + lower + upper)
 
-    def to_next(v):
+    head = pl.multiple_of(jnp.where(ascend, 0, cols - strip), LANE)
+    tail = pl.multiple_of(jnp.where(ascend, strip, 0), LANE)
+    spans = ((head, strip), (tail, cols - strip))
+
+    def halo(n, way, v):
+        at, size = spans[n]
+        if way == 0:
+            here, there, tile = rows - EDGE, rows + EDGE, lax.rem(t + 1, tiles)
+        else:
+            here, there, tile = 0, rows, lax.rem(t + tiles - 1, tiles)
         return pltpu.make_async_remote_copy(
-            src_ref=img_ref.at[v, pl.ds(rows - EDGE, EDGE)],
-            dst_ref=buf.at[v, pl.ds(rows + EDGE, EDGE), body],
-            send_sem=halo_send.at[0, v],
-            recv_sem=halo_recv.at[0, v],
-            device_id=(lax.rem(t + 1, tiles), g),
+            src_ref=img_ref.at[v, pl.ds(here, EDGE), pl.ds(at, size)],
+            dst_ref=buf.at[v, pl.ds(there, EDGE), pl.ds(pl.multiple_of(at + LANE, LANE), size)],
+            send_sem=halo_send.at[n, way, v],
+            recv_sem=halo_recv.at[n, way, v],
+            device_id=(tile, g),
             device_id_type=MESH,
         )
 
-    def to_last(v):
-        return pltpu.make_async_remote_copy(
-            src_ref=img_ref.at[v, pl.ds(0, EDGE)],
-            dst_ref=buf.at[v, pl.ds(rows, EDGE), body],
-            send_sem=halo_send.at[1, v],
-            recv_sem=halo_recv.at[1, v],
-            device_id=(lax.rem(t + tiles - 1, tiles), g),
-            device_id_type=MESH,
-        )
-
-    def sends(v, act):
+    def sends(n, v, act):
         @pl.when((t < tiles - 1) & needs(t + 1, v))
         def _():
-            act(to_next(v))
+            act(halo(n, 0, v))
 
         @pl.when((t > 0) & needs(t - 1, v))
         def _():
-            act(to_last(v))
-
-    def start_halo(v, carry):
-        sends(v, lambda c: c.start())
-        return carry
-
-    lax.fori_loop(0, visits, start_halo, 0)
+            act(halo(n, 1, v))
+
+    for n in range(2):
+        def start_halo(v, carry):
+            sends(n, v, lambda c: c.start())
+            return carry
+
+        lax.fori_loop(0, visits, start_halo, 0)
+
+    def arrive(n, v):
+        @pl.when(t > 0)
+        def _():
+            halo(n, 0, v).wait_recv()
+
+        @pl.when(t < tiles - 1)
+        def _():
+            halo(n, 1, v).wait_recv()
+
+    def ready(v, s):
+        @pl.when(s == 0)
+        def _():
+            img_copy(v).wait()
+            inv_copy(v).wait()
+            arrive(0, v)
+
+        @pl.when(s == 1)
+        def _():
+            arrive(1, v)
+
+    spot = lax.broadcasted_iota(jnp.int32, (taps, WIN), 1)
+    which = lax.broadcasted_iota(jnp.int32, (taps, WIN), 0)
+
+    def placed(ref, wanted):
+        picks = jnp.where(wanted == which, 1.0, 0.0).astype(jnp.bfloat16)
+        return jnp.dot(ref[...], picks, preferred_element_type=jnp.float32)
+
+    base_ref[0] = placed(row_ref, jnp.where(spot >= WIN - half, spot - WIN, spot) + half)
+    base_ref[1] = placed(row_ref, spot - (LANE + EDGE - half))
+    base_ref[2] = placed(col_ref, jnp.where(spot == 0, 0, WIN - spot))
 
     def one_table(k, carry):
-        def spread(which, count):
-            line = jnp.broadcast_to(base_ref[k, pl.ds(which, 1), :], (count, WIN))
+        def spread(n, count):
+            line = jnp.broadcast_to(base_ref[n, pl.ds(k, 1), :], (count, WIN))
             return pltpu.roll(line, 0, 1, stride=1, stride_axis=0)
 
         own = spread(0, rows)[:, :LANE]
@@ -179,64 +201,79 @@
         turn = lax.rem(WIN + LANE - lax.rem(at, LANE), WIN + LANE)
         return pltpu.roll(chunk, turn, 1)[:, :WIN]
 
-    ascend = g >= groups // 2
-
-    def one_pair(s, carry):
-        q = jnp.where(ascend, s, pairs - 1 - s)
-        acc[...] = jnp.zeros_like(acc)
+    def place_of(s):
+        return jnp.where(ascend, s, pairs - 1 - s)
+
+    def row_windows(v, q):
+        return [
+            window(buf, v, (q * PAIR + j) * step + LANE - half).astype(jnp.bfloat16)
+            for j in range(PAIR)
+        ]
+
+    def row_half(dst, tall, j):
+        made = jnp.dot(
+            row_tab[...].reshape(basis * rows, deep), tall[j], preferred_element_type=jnp.float32
+        )
+        dst[:, j] = made.astype(jnp.bfloat16).reshape(basis, rows, WIN)
+
+    def step_pair(src, v, on, q, dst, v_next, q_next):
+        tall = row_windows(v_next, q_next)
+        row_half(dst, tall, 0)
         col_ids = (q * PAIR + place) * step + lane
         col_coord = (2.0 * col_ids.astype(jnp.float32) + 1.0) / cols - 1.0
-
-        def one_visit(v, inner):
-            @pl.when(needs(t, v))
+        who = g * visits + v
+        shift = shift_ref[who]
+        age = lax.rem(who - first + visits_all, visits_all)
+        scale = jnp.where((age < depth_ref[0]) & on, 1.0, 0.0)
+        matched = jnp.zeros((PAIR, rows, WIN), jnp.float32)
+        for k in range(basis):
+            if k == basis // 2:
+                row_half(dst, tall, 1)
+            image = jnp.dot(
+                src[k].reshape(PAIR * rows, WIN), col_tab[k], preferred_element_type=jnp.float32
+            ).reshape(PAIR, rows, WIN)
+            c0 = coef_ref[k, 0, who]
+            c1 = coef_ref[k, 1, who]
+            c2 = coef_ref[k, 2, who]
+            matched = matched + ((c0 + c1 * col_coord) + c2 * row_coord) * image
+        weight = jnp.stack([window(inv, v, (q * PAIR + j) * step) for j in range(PAIR)])
+        inside = (col_ids >= shift) & (col_ids < shift + cols - DITHER) & (lane < step)
+        weight = weight * jnp.where(inside, scale, 0.0)
+        acc[0] += weight * matched
+        acc[1] += weight
+
+    @pl.when(twos > 0)
+    def _():
+        ready(lo, 0)
+        tall = row_windows(lo, place_of(0))
+        row_half(pass_a, tall, 0)
+        row_half(pass_a, tall, 1)
+
+    def one_pair(s, carry):
+        q = place_of(s)
+        acc[...] = jnp.zeros_like(acc)
+
+        def two_visits(i, inner):
+            va = lo + 2 * i
+            more = va + 1 < hi
+            vb = jnp.where(more, va + 1, va)
+            final = i == twos - 1
+            vn = jnp.where(final, lo, va + 2)
+            sn = jnp.where(final, jnp.minimum(s + 1, pairs - 1), s)
+
+            @pl.when(more)
             def _():
-                @pl.when(s == 0)
-                def _():
-                    img_copy(v).wait()
-                    inv_copy(v).wait()
-
-                    @pl.when(t > 0)
-                    def _():
-                        to_next(v).wait_recv()
-
-                    @pl.when(t < tiles - 1)
-                    def _():
-                        to_last(v).wait_recv()
-
-                who = g * visits + v
-                shift = shift_ref[who]
-                on = lax.rem(who - first + visits_all, visits_all) < depth_ref[0]
-                scale = jnp.where(on, 1.0, 0.0)
-                weights = []
-                for j in range(PAIR):
-                    at = (q * PAIR + j) * step
-                    tall = window(buf, v, at + LANE - (WIN - step) // 2)
-                    made = jnp.dot(
-                        row_tab[...].reshape(basis * rows, deep),
-                        tall.astype(jnp.bfloat16),
-                        preferred_element_type=jnp.float32,
-                    )
-                    passed[:, j] = made.astype(jnp.bfloat16).reshape(basis, rows, WIN)
-                    weights.append(window(inv, v, at))
-                matched = jnp.zeros((PAIR, rows, WIN), jnp.float32)
-                for k in range(basis):
-                    image = jnp.dot(
-                        passed[k].reshape(PAIR * rows, WIN),
-                        col_tab[k],
-                        preferred_element_type=jnp.float32,
-                    ).reshape(PAIR, rows, WIN)
-                    c0 = coef_ref[(who * basis + k) * 3]
-                    c1 = coef_ref[(who * basis + k) * 3 + 1]
-                    c2 = coef_ref[(who * basis + k) * 3 + 2]
-                    matched = matched + ((c0 + c1 * col_coord) + c2 * row_coord) * image
-                inside = (col_ids >= shift) & (col_ids < shift + cols - DITHER) & (lane < step)
-                weight = jnp.stack(weights) * jnp.where(inside, scale, 0.0)
-                acc[0] += weight * matched
-                acc[1] += weight
-
+                ready(vb, s)
+
+            @pl.when(jnp.logical_not(final) | (s < pairs - 1))
+            def _():
+                ready(vn, sn)
+
+            step_pair(pass_a, va, True, q, pass_b, vb, q)
+            step_pair(pass_b, vb, more, q, pass_a, vn, place_of(sn))
             return inner
 
-        lax.fori_loop(0, visits, one_visit, 0)
+        lax.fori_loop(0, twos, two_visits, 0)
 
         @pl.when(gives(g))
         def _():
@@ -287,11 +324,12 @@
         for d in range(1, groups):
             part_copy(d).wait_send()
 
-    def end_halo(v, carry):
-        sends(v, lambda c: c.wait_send())
-        return carry
-
-    lax.fori_loop(0, visits, end_halo, 0)
+    for n in range(2):
+        def end_halo(v, carry):
+            sends(n, v, lambda c: c.wait_send())
+            return carry
+
+        lax.fori_loop(0, visits, end_halo, 0)
 
 
 def local(images, inv_var, row_taps, col_taps, coeffs, dithers, depths):
@@ -304,7 +342,6 @@
     strip = cols // groups
     room = cols + WIN
     deep = rows + 2 * EDGE
-    bases = base_rows(row_taps, col_taps, rows)
     sizes = (tiles, groups, step)
 
     def run(*refs):
@@ -318,13 +355,15 @@
     return pl.pallas_call(
         run,
         out_shape=jax.ShapeDtypeStruct((rows, strip), jnp.float32),
-        in_specs=[smem, smem, smem, vmem, hbm, hbm],
+        in_specs=[smem, smem, smem, vmem, vmem, hbm, hbm],
         out_specs=vmem,
         scratch_shapes=[
             pltpu.VMEM((visits, deep, LANE + cols + WIN), jnp.bfloat16),
             pltpu.VMEM((visits, rows, room), jnp.bfloat16),
+            pltpu.VMEM((3, basis, WIN), jnp.float32),
             pltpu.VMEM((basis, rows, deep), jnp.bfloat16),
             pltpu.VMEM((basis, WIN, WIN), jnp.bfloat16),
+            pltpu.VMEM((basis, PAIR, rows, WIN), jnp.bfloat16),
             pltpu.VMEM((basis, PAIR, rows, WIN), jnp.bfloat16),
             pltpu.VMEM((2, PAIR, rows, WIN), jnp.float32),
             pltpu.VMEM((2, rows, room), jnp.float32),
@@ -332,18 +371,18 @@
             pltpu.VMEM((groups - 1, 2, rows, strip), jnp.bfloat16),
             dma((visits,)),
             dma((visits,)),
-            dma((2, visits)),
-            dma((2, visits)),
+            dma((2, 2, visits)),
+            dma((2, 2, visits)),
             dma((groups - 1,)),
             dma((groups - 1,)),
         ],
         compiler_params=pltpu.CompilerParams(
-            vmem_limit_bytes=48 * 1024 * 1024, collective_id=0, has_side_effects=True
+            vmem_limit_bytes=60 * 1024 * 1024, collective_id=0, has_side_effects=True
         ),
         cost_estimate=pl.CostEstimate(
             flops=flops, bytes_accessed=4 * visits * rows * cols, transcendentals=0
         ),
-    )(coeffs.reshape(-1), dithers, depths, bases, images, inv_var)
+    )(jnp.transpose(coeffs, (1, 2, 0)), dithers, depths, row_taps, col_taps, images, inv_var)
 
 
 def solution(mesh):

time: 67.4 us -> 51.9 us (0.77)
  Pallas kernels: 60.1 us -> 49.4 us
  local copies, waits for them, and re-layouts: 4.36 us -> 1.62 us
  other arithmetic: 1.82 us -> 0 us
    pallas_call x1, Pallas kernels: 60.1 us -> 49.4 us  [local(): pl.pallas_call(run, out_shape=jax.ShapeDtypeStruct((rows, strip), jnp.flo...]
    unnamed x6 -> x1, local copies, waits for them, and re-layouts: 4.14 us -> 1.62 us
    convert_element_type x2 -> x0, other arithmetic: 1.38 us -> none  [placed(): table.astype(jnp.float32)[:, :, None]]
where the time goes in v3:
time: 51.9 us; the launch traced here: 51.7 us
  Pallas kernels  49.4 us (95%)
  local copies, waits for them, and re-layouts  1.62 us (3%)
  between operations  0.66 us (1%)
    pallas_call x1, Pallas kernels, local(): pl.pallas_call(run, out_shape=jax.ShapeDtypeStruct((rows, strip), jnp.flo...  49.4 us
    unnamed x1, local copies, waits for them, and re-layouts  1.62 us

profile of v3, /device:TPU:28, one launch (start us, length us, event | category | flops | bytes accessed | tf_op | source)
XLA Modules:
  0.0 51.7 jit_solution(4170818413745457153)
XLA Ops:
  0.7 49.4 %shard_map.73 = f32[96,512]{1,0:T(8,128)} custom-call(f32[11,3,32]{2,1,0:T(4,128)} %bitcast.1, s32[32]{0:T(128)} %refs_1_.1, s32[1]{0:T(128)S(6)} %copy.9.refs_2_, bf16[11,41]{1,0:T(8,128)(2,1)} %refs_3_.1, bf16[11,41]{1,0:T(8,128)(2,1)} %refs_4_.1, bf16[8,96,2048]{2,1,0:T(8,128)(2,1)} %refs_5_.1, bf16[8,96,2048]{2,1,0:T(8,128)(2,1)} %refs_6_.1), custom_call_target="tpu_custom_call" | custom-call | flops 22145925120 | bytes 6291456 | tf_op jit(solution)/shard_map/pallas_call | solution.py:355
  50.0 1.6 %copy.10 = f32[96,512]{1,0:T(8,128)} copy(f32[96,512]{1,0:T(8,128)} %shard_map.73) | data formatting | bytes 393216

commit v4 on v3

--- a/solution.py
+++ b/solution.py
@@ -182,7 +182,7 @@
         own = spread(0, rows)[:, :LANE]
         above = spread(1, rows)[:, LANE:]
         both = jnp.concatenate([own, above], axis=1).astype(jnp.bfloat16)
-        row_tab[k] = both[:, :deep]
+        row_tab[pl.ds(pl.multiple_of(k * rows, 32), rows)] = both[:, :deep]
         col_tab[k] = spread(2, WIN).astype(jnp.bfloat16)
         return carry
 
@@ -191,9 +191,8 @@
 
     row_ids = t * rows + lax.broadcasted_iota(jnp.int32, (rows, LANE), 0)
     row_coord = (2.0 * row_ids.astype(jnp.float32) + 1.0) / total_rows - 1.0
-    row_coord = jnp.concatenate([row_coord] * (WIN // LANE), axis=1)[None]
-    lane = lax.broadcasted_iota(jnp.int32, (PAIR, 1, WIN), 2)
-    place = lax.broadcasted_iota(jnp.int32, (PAIR, 1, WIN), 0)
+    row_coord = jnp.concatenate([row_coord] * (WIN // LANE), axis=1)
+    lane = lax.broadcasted_iota(jnp.int32, (1, WIN), 1)
 
     def window(ref, v, at):
         base = pl.multiple_of(lax.div(at, LANE) * LANE, LANE)
@@ -210,37 +209,41 @@
             for j in range(PAIR)
         ]
 
+    cuts = 3
+    chunk = basis * rows // cuts
+
+    def row_chunk(dst, tall, j, n):
+        at = pl.ds(n * chunk, chunk)
+        made = jnp.dot(row_tab[at, :], tall[j], preferred_element_type=jnp.float32)
+        dst[j, at] = made.astype(jnp.bfloat16)
+
     def row_half(dst, tall, j):
-        made = jnp.dot(
-            row_tab[...].reshape(basis * rows, deep), tall[j], preferred_element_type=jnp.float32
-        )
-        dst[:, j] = made.astype(jnp.bfloat16).reshape(basis, rows, WIN)
+        for n in range(cuts):
+            row_chunk(dst, tall, j, n)
 
     def step_pair(src, v, on, q, dst, v_next, q_next):
         tall = row_windows(v_next, q_next)
-        row_half(dst, tall, 0)
-        col_ids = (q * PAIR + place) * step + lane
-        col_coord = (2.0 * col_ids.astype(jnp.float32) + 1.0) / cols - 1.0
         who = g * visits + v
         shift = shift_ref[who]
         age = lax.rem(who - first + visits_all, visits_all)
         scale = jnp.where((age < depth_ref[0]) & on, 1.0, 0.0)
-        matched = jnp.zeros((PAIR, rows, WIN), jnp.float32)
-        for k in range(basis):
-            if k == basis // 2:
-                row_half(dst, tall, 1)
-            image = jnp.dot(
-                src[k].reshape(PAIR * rows, WIN), col_tab[k], preferred_element_type=jnp.float32
-            ).reshape(PAIR, rows, WIN)
-            c0 = coef_ref[k, 0, who]
-            c1 = coef_ref[k, 1, who]
-            c2 = coef_ref[k, 2, who]
-            matched = matched + ((c0 + c1 * col_coord) + c2 * row_coord) * image
-        weight = jnp.stack([window(inv, v, (q * PAIR + j) * step) for j in range(PAIR)])
-        inside = (col_ids >= shift) & (col_ids < shift + cols - DITHER) & (lane < step)
-        weight = weight * jnp.where(inside, scale, 0.0)
-        acc[0] += weight * matched
-        acc[1] += weight
+        for j in range(PAIR):
+            row_half(dst, tall, j)
+            col_ids = (q * PAIR + j) * step + lane
+            col_coord = (2.0 * col_ids.astype(jnp.float32) + 1.0) / cols - 1.0
+            matched = jnp.zeros((rows, WIN), jnp.float32)
+            for k in range(basis):
+                image = jnp.dot(
+                    src[j, k * rows : (k + 1) * rows], col_tab[k], preferred_element_type=jnp.float32
+                )
+                c0 = coef_ref[k, 0, who]
+                c1 = coef_ref[k, 1, who]
+                c2 = coef_ref[k, 2, who]
+                matched = matched + ((c0 + c1 * col_coord) + c2 * row_coord) * image
+            inside = (col_ids >= shift) & (col_ids < shift + cols - DITHER) & (lane < step)
+            weight = window(inv, v, (q * PAIR + j) * step) * jnp.where(inside, scale, 0.0)
+            acc[0, j] += weight * matched
+            acc[1, j] += weight
 
     @pl.when(twos > 0)
     def _():
@@ -361,10 +364,10 @@
             pltpu.VMEM((visits, deep, LANE + cols + WIN), jnp.bfloat16),
             pltpu.VMEM((visits, rows, room), jnp.bfloat16),
             pltpu.VMEM((3, basis, WIN), jnp.float32),
-            pltpu.VMEM((basis, rows, deep), jnp.bfloat16),
+            pltpu.VMEM((basis * rows, deep), jnp.bfloat16),
             pltpu.VMEM((basis, WIN, WIN), jnp.bfloat16),
-            pltpu.VMEM((basis, PAIR, rows, WIN), jnp.bfloat16),
-            pltpu.VMEM((basis, PAIR, rows, WIN), jnp.bfloat16),
+            pltpu.VMEM((PAIR, basis * rows, WIN), jnp.bfloat16),
+            pltpu.VMEM((PAIR, basis * rows, WIN), jnp.bfloat16),
             pltpu.VMEM((2, PAIR, rows, WIN), jnp.float32),
             pltpu.VMEM((2, rows, room), jnp.float32),
             pltpu.VMEM((groups - 1, 2, rows, strip), jnp.bfloat16),
@@ -377,7 +380,7 @@
             dma((groups - 1,)),
         ],
         compiler_params=pltpu.CompilerParams(
-            vmem_limit_bytes=60 * 1024 * 1024, collective_id=0, has_side_effects=True
+            vmem_limit_bytes=57 * 1024 * 1024, collective_id=0, has_side_effects=True
         ),
         cost_estimate=pl.CostEstimate(
             flops=flops, bytes_accessed=4 * visits * rows * cols, transcendentals=0

time: 51.9 us -> 55.1 us (1.062)
  the two profiles are of different devices: /device:TPU:28 before, /device:TPU:1 now
where the time goes in v4:
time: 55.1 us; the launch traced here: 54.5 us
  Pallas kernels  52.2 us (95%)
  local copies, waits for them, and re-layouts  1.62 us (3%)
  between operations  0.66 us (1%)
    pallas_call x1, Pallas kernels, local(): pl.pallas_call(run, out_shape=jax.ShapeDtypeStruct((rows, strip), jnp.flo...  52.2 us
    unnamed x1, local copies, waits for them, and re-layouts  1.62 us

profile of v4, /device:TPU:1, one launch (start us, length us, event | category | flops | bytes accessed | tf_op | source)
XLA Modules:
  0.0 54.5 jit_solution(2453615600211451554)
XLA Ops:
  0.7 52.2 %shard_map.73 = f32[96,512]{1,0:T(8,128)} custom-call(f32[11,3,32]{2,1,0:T(4,128)} %bitcast.1, s32[32]{0:T(128)} %refs_1_.1, s32[1]{0:T(128)S(6)} %copy.9.refs_2_, bf16[11,41]{1,0:T(8,128)(2,1)} %refs_3_.1, bf16[11,41]{1,0:T(8,128)(2,1)} %refs_4_.1, bf16[8,96,2048]{2,1,0:T(8,128)(2,1)} %refs_5_.1, bf16[8,96,2048]{2,1,0:T(8,128)(2,1)} %refs_6_.1), custom_call_target="tpu_custom_call" | custom-call | flops 22145925120 | bytes 6291456 | tf_op jit(solution)/shard_map/pallas_call | solution.py:358
  52.8 1.6 %copy.10 = f32[96,512]{1,0:T(8,128)} copy(f32[96,512]{1,0:T(8,128)} %shard_map.73) | data formatting | bytes 393216

commit v5 on v3

--- a/solution.py
+++ b/solution.py
@@ -11,6 +11,7 @@
 PAIR = 2
 LANE = 128
 EDGE = 32
+BATCH = 4
 MESH = pl.DeviceIdType.MESH
 
 
@@ -108,60 +109,65 @@
     upper = jnp.where(t < tiles - 1, 1, 0)
     pl.semaphore_wait(barrier, groups - 1 + lower + upper)
 
-    head = pl.multiple_of(jnp.where(ascend, 0, cols - strip), LANE)
-    tail = pl.multiple_of(jnp.where(ascend, strip, 0), LANE)
-    spans = ((head, strip), (tail, cols - strip))
-
-    def halo(n, way, v):
-        at, size = spans[n]
+    def halo(n, way, b):
+        at = pl.multiple_of(jnp.where(ascend, n, groups - 1 - n) * strip, LANE)
         if way == 0:
             here, there, tile = rows - EDGE, rows + EDGE, lax.rem(t + 1, tiles)
         else:
             here, there, tile = 0, rows, lax.rem(t + tiles - 1, tiles)
+        some = pl.ds(b * BATCH, BATCH)
+        to = pl.ds(pl.multiple_of(at + LANE, LANE), strip)
         return pltpu.make_async_remote_copy(
-            src_ref=img_ref.at[v, pl.ds(here, EDGE), pl.ds(at, size)],
-            dst_ref=buf.at[v, pl.ds(there, EDGE), pl.ds(pl.multiple_of(at + LANE, LANE), size)],
-            send_sem=halo_send.at[n, way, v],
-            recv_sem=halo_recv.at[n, way, v],
+            src_ref=img_ref.at[some, pl.ds(here, EDGE), pl.ds(at, strip)],
+            dst_ref=buf.at[some, pl.ds(there, EDGE), to],
+            send_sem=halo_send.at[n, way, b],
+            recv_sem=halo_recv.at[n, way, b],
             device_id=(tile, g),
             device_id_type=MESH,
         )
 
-    def sends(n, v, act):
-        @pl.when((t < tiles - 1) & needs(t + 1, v))
-        def _():
-            act(halo(n, 0, v))
-
-        @pl.when((t > 0) & needs(t - 1, v))
-        def _():
-            act(halo(n, 1, v))
-
-    for n in range(2):
-        def start_halo(v, carry):
-            sends(n, v, lambda c: c.start())
+    def needs_any(tile, b):
+        found = needs(tile, b * BATCH)
+        for r in range(1, BATCH):
+            found = found | needs(tile, b * BATCH + r)
+        return found
+
+    def sends(n, b, act):
+        @pl.when((t < tiles - 1) & needs_any(t + 1, b))
+        def _():
+            act(halo(n, 0, b))
+
+        @pl.when((t > 0) & needs_any(t - 1, b))
+        def _():
+            act(halo(n, 1, b))
+
+    def start_halo(n):
+        def one_batch(b, carry):
+            sends(n, b, lambda c: c.start())
             return carry
 
-        lax.fori_loop(0, visits, start_halo, 0)
-
-    def arrive(n, v):
-        @pl.when(t > 0)
-        def _():
-            halo(n, 0, v).wait_recv()
-
-        @pl.when(t < tiles - 1)
-        def _():
-            halo(n, 1, v).wait_recv()
+        lax.fori_loop(0, visits // BATCH, one_batch, 0)
+
+    start_halo(0)
+    start_halo(1)
 
     def ready(v, s):
         @pl.when(s == 0)
         def _():
             img_copy(v).wait()
             inv_copy(v).wait()
-            arrive(0, v)
-
-        @pl.when(s == 1)
-        def _():
-            arrive(1, v)
+
+        @pl.when((s < groups) & ((v == lo) | (lax.rem(v, BATCH) == 0)))
+        def _():
+            b = lax.div(v, BATCH)
+
+            @pl.when(t > 0)
+            def _():
+                halo(s, 0, b).wait_recv()
+
+            @pl.when(t < tiles - 1)
+            def _():
+                halo(s, 1, b).wait_recv()
 
     spot = lax.broadcasted_iota(jnp.int32, (taps, WIN), 1)
     which = lax.broadcasted_iota(jnp.int32, (taps, WIN), 0)
@@ -253,6 +259,10 @@
         q = place_of(s)
         acc[...] = jnp.zeros_like(acc)
 
+        @pl.when(s + 2 < groups)
+        def _():
+            start_halo(s + 2)
+
         def two_visits(i, inner):
             va = lo + 2 * i
             more = va + 1 < hi
@@ -324,12 +334,15 @@
         for d in range(1, groups):
             part_copy(d).wait_send()
 
-    for n in range(2):
-        def end_halo(v, carry):
-            sends(n, v, lambda c: c.wait_send())
-            return carry
-
-        lax.fori_loop(0, visits, end_halo, 0)
+    def end_halo(n, carry):
+        def one_batch(b, inner):
+            sends(n, b, lambda c: c.wait_send())
+            return inner
+
+        lax.fori_loop(0, visits // BATCH, one_batch, 0)
+        return carry
+
+    lax.fori_loop(0, groups, end_halo, 0)
 
 
 def local(images, inv_var, row_taps, col_taps, coeffs, dithers, depths):
@@ -371,13 +384,13 @@
             pltpu.VMEM((groups - 1, 2, rows, strip), jnp.bfloat16),
             dma((visits,)),
             dma((visits,)),
-            dma((2, 2, visits)),
-            dma((2, 2, visits)),
+            dma((groups, 2, visits // BATCH)),
+            dma((groups, 2, visits // BATCH)),
             dma((groups - 1,)),
             dma((groups - 1,)),
         ],
         compiler_params=pltpu.CompilerParams(
-            vmem_limit_bytes=60 * 1024 * 1024, collective_id=0, has_side_effects=True
+            vmem_limit_bytes=55 * 1024 * 1024, collective_id=0, has_side_effects=True
         ),
         cost_estimate=pl.CostEstimate(
             flops=flops, bytes_accessed=4 * visits * rows * cols, transcendentals=0

time: 51.9 us -> 50.4 us (0.971)
  the two profiles are of different devices: /device:TPU:28 before, /device:TPU:1 now
where the time goes in v5:
time: 50.4 us; the launch traced here: 50.2 us
  Pallas kernels  47.9 us (95%)
  local copies, waits for them, and re-layouts  1.62 us (3%)
  between operations  0.66 us (1%)
    pallas_call x1, Pallas kernels, local(): pl.pallas_call(run, out_shape=jax.ShapeDtypeStruct((rows, strip), jnp.flo...  47.9 us
    unnamed x1, local copies, waits for them, and re-layouts  1.62 us

profile of v5, /device:TPU:1, one launch (start us, length us, event | category | flops | bytes accessed | tf_op | source)
XLA Modules:
  0.0 50.2 jit_solution(2698571336493991090)
XLA Ops:
  0.7 47.9 %shard_map.73 = f32[96,512]{1,0:T(8,128)} custom-call(f32[11,3,32]{2,1,0:T(4,128)} %bitcast.1, s32[32]{0:T(128)} %refs_1_.1, s32[1]{0:T(128)S(6)} %copy.9.refs_2_, bf16[11,41]{1,0:T(8,128)(2,1)} %refs_3_.1, bf16[11,41]{1,0:T(8,128)(2,1)} %refs_4_.1, bf16[8,96,2048]{2,1,0:T(8,128)(2,1)} %refs_5_.1, bf16[8,96,2048]{2,1,0:T(8,128)(2,1)} %refs_6_.1), custom_call_target="tpu_custom_call" | custom-call | flops 22145925120 | bytes 6291456 | tf_op jit(solution)/shard_map/pallas_call | solution.py:368
  48.6 1.6 %copy.10 = f32[96,512]{1,0:T(8,128)} copy(f32[96,512]{1,0:T(8,128)} %shard_map.73) | data formatting | bytes 393216

commit v6 on v5

--- a/solution.py
+++ b/solution.py
@@ -180,9 +180,9 @@
     base_ref[1] = placed(row_ref, spot - (LANE + EDGE - half))
     base_ref[2] = placed(col_ref, jnp.where(spot == 0, 0, WIN - spot))
 
-    def one_table(k, carry):
+    for k in range(basis):
         def spread(n, count):
-            line = jnp.broadcast_to(base_ref[n, pl.ds(k, 1), :], (count, WIN))
+            line = jnp.broadcast_to(base_ref[n, k : k + 1, :], (count, WIN))
             return pltpu.roll(line, 0, 1, stride=1, stride_axis=0)
 
         own = spread(0, rows)[:, :LANE]
@@ -190,9 +190,7 @@
         both = jnp.concatenate([own, above], axis=1).astype(jnp.bfloat16)
         row_tab[k] = both[:, :deep]
         col_tab[k] = spread(2, WIN).astype(jnp.bfloat16)
-        return carry
-
-    lax.fori_loop(0, basis, one_table, 0)
+
     flat[...] = jnp.zeros_like(flat)
 
     row_ids = t * rows + lax.broadcasted_iota(jnp.int32, (rows, LANE), 0)
@@ -211,20 +209,25 @@
         return jnp.where(ascend, s, pairs - 1 - s)
 
     def row_windows(v, q):
-        return [
-            window(buf, v, (q * PAIR + j) * step + LANE - half).astype(jnp.bfloat16)
-            for j in range(PAIR)
-        ]
-
-    def row_half(dst, tall, j):
+        return jnp.concatenate(
+            [
+                window(buf, v, (q * PAIR + j) * step + LANE - half).astype(jnp.bfloat16)
+                for j in range(PAIR)
+            ],
+            axis=1,
+        )
+
+    def row_part(dst, tall, k0, k1):
         made = jnp.dot(
-            row_tab[...].reshape(basis * rows, deep), tall[j], preferred_element_type=jnp.float32
-        )
-        dst[:, j] = made.astype(jnp.bfloat16).reshape(basis, rows, WIN)
+            row_tab[k0:k1].reshape((k1 - k0) * rows, deep), tall, preferred_element_type=jnp.float32
+        ).astype(jnp.bfloat16)
+        for j in range(PAIR):
+            dst[k0:k1, j] = made[:, j * WIN : (j + 1) * WIN].reshape(k1 - k0, rows, WIN)
 
     def step_pair(src, v, on, q, dst, v_next, q_next):
         tall = row_windows(v_next, q_next)
-        row_half(dst, tall, 0)
+        cut = basis // 2
+        row_part(dst, tall, 0, cut)
         col_ids = (q * PAIR + place) * step + lane
         col_coord = (2.0 * col_ids.astype(jnp.float32) + 1.0) / cols - 1.0
         who = g * visits + v
@@ -232,16 +235,24 @@
         age = lax.rem(who - first + visits_all, visits_all)
         scale = jnp.where((age < depth_ref[0]) & on, 1.0, 0.0)
         matched = jnp.zeros((PAIR, rows, WIN), jnp.float32)
-        for k in range(basis):
-            if k == basis // 2:
-                row_half(dst, tall, 1)
-            image = jnp.dot(
+        def basis_image(k):
+            return jnp.dot(
                 src[k].reshape(PAIR * rows, WIN), col_tab[k], preferred_element_type=jnp.float32
             ).reshape(PAIR, rows, WIN)
+
+        def spatial(k):
             c0 = coef_ref[k, 0, who]
             c1 = coef_ref[k, 1, who]
             c2 = coef_ref[k, 2, who]
-            matched = matched + ((c0 + c1 * col_coord) + c2 * row_coord) * image
+            return (c0 + c1 * col_coord) + c2 * row_coord
+
+        for k in range(0, basis, 2):
+            if k == cut - cut % 2:
+                row_part(dst, tall, cut, basis)
+            pair = [kk for kk in (k, k + 1) if kk < basis]
+            both = [basis_image(kk) for kk in pair]
+            for kk, image in zip(pair, both):
+                matched = matched + spatial(kk) * image
         weight = jnp.stack([window(inv, v, (q * PAIR + j) * step) for j in range(PAIR)])
         inside = (col_ids >= shift) & (col_ids < shift + cols - DITHER) & (lane < step)
         weight = weight * jnp.where(inside, scale, 0.0)
@@ -252,8 +263,7 @@
     def _():
         ready(lo, 0)
         tall = row_windows(lo, place_of(0))
-        row_half(pass_a, tall, 0)
-        row_half(pass_a, tall, 1)
+        row_part(pass_a, tall, 0, basis)
 
     def one_pair(s, carry):
         q = place_of(s)

time: 50.4 us -> 52.1 us (1.034)
  Pallas kernels: 47.9 us -> 49.6 us
    pallas_call x1, Pallas kernels: 47.9 us -> 49.6 us  [local(): pl.pallas_call(run, out_shape=jax.ShapeDtypeStruct((rows, strip), jnp.flo...]
where the time goes in v6:
time: 52.1 us; the launch traced here: 51.9 us
  Pallas kernels  49.6 us (95%)
  local copies, waits for them, and re-layouts  1.62 us (3%)
  between operations  0.66 us (1%)
    pallas_call x1, Pallas kernels, local(): pl.pallas_call(run, out_shape=jax.ShapeDtypeStruct((rows, strip), jnp.flo...  49.6 us
    unnamed x1, local copies, waits for them, and re-layouts  1.62 us

profile of v6, /device:TPU:1, one launch (start us, length us, event | category | flops | bytes accessed | tf_op | source)
XLA Modules:
  0.0 51.9 jit_solution(5190685167430824687)
XLA Ops:
  0.7 49.6 %shard_map.73 = f32[96,512]{1,0:T(8,128)} custom-call(f32[11,3,32]{2,1,0:T(4,128)} %bitcast.1, s32[32]{0:T(128)} %refs_1_.1, s32[1]{0:T(128)S(6)} %copy.9.refs_2_, bf16[11,41]{1,0:T(8,128)(2,1)} %refs_3_.1, bf16[11,41]{1,0:T(8,128)(2,1)} %refs_4_.1, bf16[8,96,2048]{2,1,0:T(8,128)(2,1)} %refs_5_.1, bf16[8,96,2048]{2,1,0:T(8,128)(2,1)} %refs_6_.1), custom_call_target="tpu_custom_call" | custom-call | flops 22145925120 | bytes 6291456 | tf_op jit(solution)/shard_map/pallas_call | solution.py:378
  50.3 1.6 %copy.10 = f32[96,512]{1,0:T(8,128)} copy(f32[96,512]{1,0:T(8,128)} %shard_map.73) | data formatting | bytes 393216

commit v7 on v5

--- a/solution.py
+++ b/solution.py
@@ -19,7 +19,7 @@
     sizes,
     coef_ref, shift_ref, depth_ref, row_ref, col_ref, img_ref, inv_ref,
     out_ref,
-    buf, inv, base_ref, row_tab, col_tab, pass_a, pass_b, acc, flat, outgo, income,
+    buf, inv, base_ref, row_tab, col_tab, pass_a, pass_b, acc, flat, total, outgo, income,
     img_sem, inv_sem, halo_send, halo_recv, part_send, part_recv,
 ):
     tiles, groups, step = sizes
@@ -155,7 +155,6 @@
         @pl.when(s == 0)
         def _():
             img_copy(v).wait()
-            inv_copy(v).wait()
 
         @pl.when((s < groups) & ((v == lo) | (lax.rem(v, BATCH) == 0)))
         def _():
@@ -245,8 +244,43 @@
         weight = jnp.stack([window(inv, v, (q * PAIR + j) * step) for j in range(PAIR)])
         inside = (col_ids >= shift) & (col_ids < shift + cols - DITHER) & (lane < step)
         weight = weight * jnp.where(inside, scale, 0.0)
-        acc[0] += weight * matched
-        acc[1] += weight
+        acc[...] += weight * matched
+
+    def part_copy(n, d):
+        return pltpu.make_async_remote_copy(
+            src_ref=outgo.at[n, d - 1],
+            dst_ref=income.at[n, d - 1],
+            send_sem=part_send.at[n, d - 1],
+            recv_sem=part_recv.at[n, d - 1],
+            device_id=(t, lax.rem(g + d, groups)),
+            device_id_type=MESH,
+        )
+
+    total[...] = jnp.zeros_like(total)
+
+    def add_weight(v, carry):
+        inv_copy(v).wait()
+        who = g * visits + v
+        shift = shift_ref[who]
+        age = lax.rem(who - first + visits_all, visits_all)
+        scale = jnp.where(age < depth_ref[0], 1.0, 0.0)
+        for c in range(groups):
+            at = c * strip
+            ids = at + lax.broadcasted_iota(jnp.int32, (1, strip), 1)
+            inside = (ids >= shift) & (ids < shift + cols - DITHER)
+            here = inv[v, :, at : at + strip].astype(jnp.float32)
+            total[:, at : at + strip] += here * jnp.where(inside, scale, 0.0)
+        return carry
+
+    lax.fori_loop(lo, hi, add_weight, 0)
+
+    @pl.when(gives(g))
+    def _():
+        for d in range(1, groups):
+            c = lax.rem(g + d, groups)
+            here = total[:, pl.ds(pl.multiple_of(c * strip, LANE), strip)]
+            outgo[1, d - 1] = here.astype(jnp.bfloat16)
+            part_copy(1, d).start()
 
     @pl.when(twos > 0)
     def _():
@@ -290,32 +324,19 @@
             for j in range(PAIR):
                 at = (q * PAIR + j) * step
                 base = pl.multiple_of(lax.div(at, LANE) * LANE, LANE)
-                for n in range(2):
-                    part = acc[n, j]
-                    part = jnp.concatenate([part, jnp.zeros((rows, LANE), jnp.float32)], axis=1)
-                    flat[n, :, pl.ds(base, WIN + LANE)] += pltpu.roll(part, lax.rem(at, LANE), 1)
+                part = jnp.concatenate([acc[j], jnp.zeros((rows, LANE), jnp.float32)], axis=1)
+                flat[:, pl.ds(base, WIN + LANE)] += pltpu.roll(part, lax.rem(at, LANE), 1)
 
             c = jnp.where(ascend, s - 1, pairs - 1 - s)
 
             @pl.when((s > 0) & (c != g))
             def _():
                 d = lax.rem(c - g + groups, groups)
-                for n in range(2):
-                    here = flat[n, :, pl.ds(pl.multiple_of(c * strip, LANE), strip)]
-                    outgo[d - 1, n] = here.astype(jnp.bfloat16)
-                part_copy(d).start()
-
-        return carry
-
-    def part_copy(d):
-        return pltpu.make_async_remote_copy(
-            src_ref=outgo.at[d - 1],
-            dst_ref=income.at[d - 1],
-            send_sem=part_send.at[d - 1],
-            recv_sem=part_recv.at[d - 1],
-            device_id=(t, lax.rem(g + d, groups)),
-            device_id_type=MESH,
-        )
+                here = flat[:, pl.ds(pl.multiple_of(c * strip, LANE), strip)]
+                outgo[0, d - 1] = here.astype(jnp.bfloat16)
+                part_copy(0, d).start()
+
+        return carry
 
     lax.fori_loop(0, pairs, one_pair, 0)
 
@@ -323,16 +344,17 @@
     for d in range(1, groups):
         @pl.when(gives(lax.rem(g - d + groups, groups)))
         def _():
-            part_copy(d).wait_recv()
-            for n in range(2):
-                flat[n, :, mine] += income[d - 1, n].astype(jnp.float32)
-
-    out_ref[...] = flat[0, :, mine] / (1.0 + flat[1, :, mine])
+            for n, held in enumerate((flat, total)):
+                part_copy(n, d).wait_recv()
+                held[:, mine] += income[n, d - 1].astype(jnp.float32)
+
+    out_ref[...] = flat[:, mine] / (1.0 + total[:, mine])
 
     @pl.when(gives(g))
     def _():
-        for d in range(1, groups):
-            part_copy(d).wait_send()
+        for n in range(2):
+            for d in range(1, groups):
+                part_copy(n, d).wait_send()
 
     def end_halo(n, carry):
         def one_batch(b, inner):
@@ -378,19 +400,20 @@
             pltpu.VMEM((basis, WIN, WIN), jnp.bfloat16),
             pltpu.VMEM((basis, PAIR, rows, WIN), jnp.bfloat16),
             pltpu.VMEM((basis, PAIR, rows, WIN), jnp.bfloat16),
-            pltpu.VMEM((2, PAIR, rows, WIN), jnp.float32),
-            pltpu.VMEM((2, rows, room), jnp.float32),
-            pltpu.VMEM((groups - 1, 2, rows, strip), jnp.bfloat16),
-            pltpu.VMEM((groups - 1, 2, rows, strip), jnp.bfloat16),
+            pltpu.VMEM((PAIR, rows, WIN), jnp.float32),
+            pltpu.VMEM((rows, room), jnp.float32),
+            pltpu.VMEM((rows, cols), jnp.float32),
+            pltpu.VMEM((2, groups - 1, rows, strip), jnp.bfloat16),
+            pltpu.VMEM((2, groups - 1, rows, strip), jnp.bfloat16),
             dma((visits,)),
             dma((visits,)),
             dma((groups, 2, visits // BATCH)),
             dma((groups, 2, visits // BATCH)),
-            dma((groups - 1,)),
-            dma((groups - 1,)),
+            dma((2, groups - 1)),
+            dma((2, groups - 1)),
         ],
         compiler_params=pltpu.CompilerParams(
-            vmem_limit_bytes=55 * 1024 * 1024, collective_id=0, has_side_effects=True
+            vmem_limit_bytes=52 * 1024 * 1024, collective_id=0, has_side_effects=True
         ),
         cost_estimate=pl.CostEstimate(
             flops=flops, bytes_accessed=4 * visits * rows * cols, transcendentals=0

time: 50.4 us -> 49.7 us (0.986)
  Pallas kernels: 47.9 us -> 45.4 us
  local copies, waits for them, and re-layouts: 1.62 us -> 3.43 us
    pallas_call x1, Pallas kernels: 47.9 us -> 45.4 us  [local(): pl.pallas_call(run, out_shape=jax.ShapeDtypeStruct((rows, strip), jnp.flo...]
    unnamed x1 -> x9, local copies, waits for them, and re-layouts: 1.62 us -> 3.43 us
where the time goes in v7:
time: 49.7 us; the launch traced here: 49.5 us
  Pallas kernels  45.4 us (91%)
  local copies, waits for them, and re-layouts  3.43 us (7%)
  between operations  0.67 us (1%)
    pallas_call x1, Pallas kernels, local(): pl.pallas_call(run, out_shape=jax.ShapeDtypeStruct((rows, strip), jnp.flo...  45.4 us
    unnamed x9, local copies, waits for them, and re-layouts  3.43 us

profile of v7, /device:TPU:1, one launch (start us, length us, event | category | flops | bytes accessed | tf_op | source)
XLA Modules:
  0.0 49.5 jit_solution(1917733649925793590)
XLA Ops:
  0.7 0.0 copy-start
  0.7 0.7 %copy-done = f32[32,11,3]{0,2,1:T(4,128)S(1)} copy-done((f32[32,11,3]{0,2,1:T(4,128)S(1)}, f32[32,11,3]{0,2,1:T(4,128)}, u32[]{:S(2)}) %copy-start) | copy-done | bytes 4248
  1.4 0.0 copy-start.1
  1.4 0.7 %copy-done.1 = bf16[11,41]{1,0:T(8,128)(2,1)S(1)} copy-done((bf16[11,41]{1,0:T(8,128)(2,1)S(1)}, bf16[11,41]{1,0:T(8,128)(2,1)}, u32[]{:S(2)}) %copy-start.1) | copy-done | bytes 926
  2.1 0.0 copy-start.2
  2.1 0.7 %copy-done.2 = bf16[11,41]{1,0:T(8,128)(2,1)S(1)} copy-done((bf16[11,41]{1,0:T(8,128)(2,1)S(1)}, bf16[11,41]{1,0:T(8,128)(2,1)}, u32[]{:S(2)}) %copy-start.2) | copy-done | bytes 926
  2.8 0.0 copy-start.3
  2.8 0.7 %copy-done.3 = s32[32]{0:T(128)S(1)} copy-done((s32[32]{0:T(128)S(1)}, s32[32]{0:T(128)}, u32[]{:S(2)}) %copy-start.3) | copy-done | bytes 152
  3.4 45.4 %shard_map.73 = f32[96,512]{1,0:T(8,128)S(1)} custom-call(f32[11,3,32]{2,1,0:T(4,128)S(1)} %bitcast.1, s32[32]{0:T(128)S(1)} %copy-done.3, s32[1]{0:T(128)S(6)} %copy.9.refs_2_, bf16[11,41]{1,0:T(8,128)(2,1)S(1)} %copy-done.1, bf16[11,41]{1,0:T(8,128)(2,1)S(1)} %copy-done.2, bf16[8,96,2048]{2,1,0:T(8,128)(2,1)} %refs_5_.1, bf16[8,96,2048]{2,1,0:T(8,128)(2,1)} %refs_6_.1), custom_call_target="tpu_custom_call" | custom-call | flops 22145925120 | bytes 6291456 | tf_op jit(solution)/shard_map/pallas_call | solution.py:390
  48.8 0.7 %copy.10 = f32[96,512]{1,0:T(8,128)} copy(f32[96,512]{1,0:T(8,128)S(1)} %shard_map.73) | data formatting | bytes 393216
Async XLA Ops:
  0.7 0.7 %copy-start = (f32[32,11,3]{0,2,1:T(4,128)S(1)}, f32[32,11,3]{0,2,1:T(4,128)}, u32[]{:S(2)}) copy-start(f32[32,11,3]{0,2,1:T(4,128)} %param.11) | copy-start | bytes 12676
  1.4 0.7 %copy-start.1 = (bf16[11,41]{1,0:T(8,128)(2,1)S(1)}, bf16[11,41]{1,0:T(8,128)(2,1)}, u32[]{:S(2)}) copy-start(bf16[11,41]{1,0:T(8,128)(2,1)} %refs_3_.1) | copy-start | bytes 2710
  2.1 0.7 %copy-start.2 = (bf16[11,41]{1,0:T(8,128)(2,1)S(1)}, bf16[11,41]{1,0:T(8,128)(2,1)}, u32[]{:S(2)}) copy-start(bf16[11,41]{1,0:T(8,128)(2,1)} %refs_4_.1) | copy-start | bytes 2710
  2.8 0.7 %copy-start.3 = (s32[32]{0:T(128)S(1)}, s32[32]{0:T(128)}, u32[]{:S(2)}) copy-start(s32[32]{0:T(128)} %refs_1_.1) | copy-start | bytes 388

commit v8 on v7

--- a/solution.py
+++ b/solution.py
@@ -149,7 +149,6 @@
         lax.fori_loop(0, visits // BATCH, one_batch, 0)
 
     start_halo(0)
-    start_halo(1)
 
     def ready(v, s):
         @pl.when(s == 0)
@@ -273,6 +272,7 @@
         return carry
 
     lax.fori_loop(lo, hi, add_weight, 0)
+    start_halo(1)
 
     @pl.when(gives(g))
     def _():
@@ -413,7 +413,7 @@
             dma((2, groups - 1)),
         ],
         compiler_params=pltpu.CompilerParams(
-            vmem_limit_bytes=52 * 1024 * 1024, collective_id=0, has_side_effects=True
+            vmem_limit_bytes=57 * 1024 * 1024, collective_id=0, has_side_effects=True
         ),
         cost_estimate=pl.CostEstimate(
             flops=flops, bytes_accessed=4 * visits * rows * cols, transcendentals=0

time: 49.7 us -> 48.7 us (0.980)
  local copies, waits for them, and re-layouts: 3.43 us -> 1.62 us
  Pallas kernels: 45.4 us -> 46.2 us
    unnamed x9 -> x1, local copies, waits for them, and re-layouts: 3.43 us -> 1.62 us
    pallas_call x1, Pallas kernels: 45.4 us -> 46.2 us  [local(): pl.pallas_call(run, out_shape=jax.ShapeDtypeStruct((rows, strip), jnp.flo...]
where the time goes in v8:
time: 48.7 us; the launch traced here: 48.4 us
  Pallas kernels  46.2 us (95%)
  local copies, waits for them, and re-layouts  1.62 us (3%)
  between operations  0.66 us (1%)
    pallas_call x1, Pallas kernels, local(): pl.pallas_call(run, out_shape=jax.ShapeDtypeStruct((rows, strip), jnp.flo...  46.2 us
    unnamed x1, local copies, waits for them, and re-layouts  1.62 us

profile of v8, /device:TPU:1, one launch (start us, length us, event | category | flops | bytes accessed | tf_op | source)
XLA Modules:
  0.0 48.4 jit_solution(18333577832412277987)
XLA Ops:
  0.7 46.2 %shard_map.73 = f32[96,512]{1,0:T(8,128)} custom-call(f32[11,3,32]{2,1,0:T(4,128)} %bitcast.1, s32[32]{0:T(128)} %refs_1_.1, s32[1]{0:T(128)S(6)} %copy.9.refs_2_, bf16[11,41]{1,0:T(8,128)(2,1)} %refs_3_.1, bf16[11,41]{1,0:T(8,128)(2,1)} %refs_4_.1, bf16[8,96,2048]{2,1,0:T(8,128)(2,1)} %refs_5_.1, bf16[8,96,2048]{2,1,0:T(8,128)(2,1)} %refs_6_.1), custom_call_target="tpu_custom_call" | custom-call | flops 22145925120 | bytes 6291456 | tf_op jit(solution)/shard_map/pallas_call | solution.py:390
  46.8 1.6 %copy.10 = f32[96,512]{1,0:T(8,128)} copy(f32[96,512]{1,0:T(8,128)} %shard_map.73) | data formatting | bytes 393216
